TPU v7x, 512 devices: a whole 4x4x16 slice. The times are simulated.
512 devices in a mesh: sp: 32 (over x_lo, z), fsdp: 8 (over y, core), dp: 2 (over x_hi).
Axes of the slice: x: 4 (x_hi: 2, x_lo: 2; x = x_hi * 2 + x_lo), y: 4, z: 16, core: 2. Of those that a mesh axis runs over, the one named last changes fastest.
Arguments:
- tokens: bfloat16 [16, 4096, 1152], P(('fsdp', 'dp'), 'sp'), may hold values from -6 to 6
- key_proj: bfloat16 [16, 4096, 4096], P(('fsdp', 'dp'), 'sp'), may hold values from -6 to 6
- key_cot: bfloat16 [16, 4096, 4096], P(('fsdp', 'dp'), None, 'sp'), may hold values from -6 to 6
- gate_cot: bfloat16 [16, 4096, 4096], P(('fsdp', 'dp'), None, 'sp'), may hold values from -6 to 6
- key_weight: bfloat16 [1152, 4096], P('fsdp'), may hold values from -0.1875 to 0.1875
- gate_down: bfloat16 [1152, 128], P('fsdp'), may hold values from -0.1875 to 0.1875
- gate_up: bfloat16 [128, 4096], P('fsdp'), may hold values from -0.5 to 0.5
- gate_bias: float32 [4096], replicated, may hold values from -4 to 4
- conv_weight: bfloat16 [4, 4096], replicated, may hold values from -3 to 3
Outputs:
- input_grad: bfloat16 [16, 4096, 1152], P(('fsdp', 'dp'), 'sp')
- down_grad: float32 [1152, 128], P('fsdp')
- up_grad: float32 [128, 4096], P('fsdp', 'sp')
- conv_grad: float32 [4, 4096], P(None, 'fsdp')
- bias_grad: float32 [4096], P('fsdp')
All inputs are finite; a program needn't handle non-finite values.
Results may differ from a plain program's by a relative error of at most 0.007.
Values may be sent and summed in bfloat16 or wider, within the bound.
No kernel may reach another device: no remote copies, remote signals or barrier semaphores. Data moves between devices by JAX's collectives and lax.ppermute only.
A program may use at most 64 MiB of HBM per device.

v0:
```python
import jax
import jax.numpy as jnp
from jax import lax
from jax.sharding import PartitionSpec as P

CONV = 4


def shifted(block, axis, distance):
    devices = range(lax.axis_size(axis))
    route = [(i - distance, i) for i in devices if i - distance in devices]
    return lax.ppermute(block, axis, route)


def silu_slope(values):
    squashed = jax.nn.sigmoid(values)
    return squashed * (1.0 + values * (1.0 - squashed))


def causal_conv(earlier, conv_taps, count):
    margin = CONV - 1
    return sum(
        (
            conv_taps[offset] * earlier[margin - offset : margin - offset + count]
            for offset in range(CONV)
        )
    )


def per_device(
    tokens, key_proj, key_cot, gate_cot, key_weight, gate_down, gate_up, gate_bias, conv_weight
):
    key_seq, gate_seq = (
        lax.all_to_all(key_cot, "sp", split_axis=1, concat_axis=2, tiled=True),
        lax.all_to_all(gate_cot, "sp", split_axis=1, concat_axis=2, tiled=True),
    )
    length = tokens.shape[1]
    margin = CONV - 1
    conv_taps = conv_weight.astype(jnp.float32)
    inputs = tokens[0]
    projected = key_proj[0]
    fsdp_at = lax.axis_index("fsdp")
    sp_at = lax.axis_index("sp")
    head_cols = key_cot.shape[2]
    earlier_rows = shifted(projected[length - margin :], "sp", 1)
    earlier = jnp.concatenate([earlier_rows, projected], axis=0).astype(jnp.float32)
    conv_out = causal_conv(earlier, conv_taps, length)
    slope_grad = (key_seq[0].astype(jnp.float32) * silu_slope(conv_out)).astype(jnp.bfloat16)
    following = shifted(slope_grad[:margin], "sp", -1)
    later_rows = jnp.concatenate([slope_grad, following], axis=0).astype(jnp.float32)
    proj_grad = sum(
        (conv_taps[offset] * later_rows[offset : offset + length] for offset in range(CONV))
    ).astype(jnp.bfloat16)
    conv_term = jnp.stack(
        [
            jnp.sum(
                later_rows[:length] * earlier[margin - offset : margin - offset + length], axis=0
            )
            for offset in range(CONV)
        ]
    )
    key_full, down_full, up_full = (
        lax.all_gather(key_weight, "fsdp", axis=0, tiled=True),
        lax.all_gather(gate_down, "fsdp", axis=0, tiled=True),
        lax.all_gather(gate_up, "fsdp", axis=0, tiled=True),
    )
    latent = jnp.dot(inputs, down_full, preferred_element_type=jnp.float32).astype(jnp.bfloat16)
    logits = jnp.dot(latent, up_full, preferred_element_type=jnp.float32) + gate_bias
    gate_grad = (-gate_seq[0].astype(jnp.float32) * jax.nn.sigmoid(logits)).astype(jnp.bfloat16)
    bias_term = jnp.sum(gate_grad.astype(jnp.float32), axis=0)
    up_term = jnp.dot(latent.T, gate_grad, preferred_element_type=jnp.float32)
    latent_grad = jnp.dot(gate_grad, up_full.T, preferred_element_type=jnp.float32).astype(
        jnp.bfloat16
    )
    down_term = jnp.dot(inputs.T, latent_grad, preferred_element_type=jnp.float32)
    side_part = jnp.dot(latent_grad, down_full.T, preferred_element_type=jnp.float32)
    main_part = jnp.dot(proj_grad, key_full.T, preferred_element_type=jnp.float32)
    input_grad = (main_part + side_part).astype(jnp.bfloat16)[None]
    grad_scale = float(
        lax.axis_size("sp") * lax.axis_size("fsdp") * lax.axis_size("dp") * length
    ) ** (-0.5)
    rows_down = gate_down.shape[0]
    rows_up = gate_up.shape[0]
    owned_cols = conv_weight.shape[1] // lax.axis_size("fsdp")
    down_sum, up_sum, conv_sum, bias_sum = lax.psum(
        (down_term, up_term, conv_term, bias_term), ("sp", "fsdp", "dp")
    )
    down_own = lax.dynamic_slice_in_dim(down_sum, fsdp_at * rows_down, rows_down, 0)
    up_own = lax.dynamic_slice_in_dim(up_sum, fsdp_at * rows_up, rows_up, 0)
    conv_own = lax.dynamic_slice_in_dim(conv_sum, fsdp_at * owned_cols, owned_cols, 1)
    bias_own = lax.dynamic_slice_in_dim(bias_sum, fsdp_at * owned_cols, owned_cols, 0)
    up_head = lax.dynamic_slice_in_dim(up_own, sp_at * head_cols, head_cols, 1)
    return (
        input_grad,
        down_own * grad_scale,
        up_head * grad_scale,
        conv_own * grad_scale,
        bias_own * grad_scale,
    )


def solution(mesh):
    return jax.shard_map(
        per_device,
        mesh=mesh,
        in_specs=(
            P(("fsdp", "dp"), "sp", None),
            P(("fsdp", "dp"), "sp", None),
            P(("fsdp", "dp"), None, "sp"),
            P(("fsdp", "dp"), None, "sp"),
            P("fsdp", None),
            P("fsdp", None),
            P("fsdp", None),
            P(),
            P(),
        ),
        out_specs=(
            P(("fsdp", "dp"), "sp", None),
            P("fsdp", None),
            P("fsdp", "sp"),
            P(None, "fsdp"),
            P("fsdp"),
        ),
        check_vma=False,
    )
```

profile of v0, /device:TPU:1, one launch (start us, length us, event | category | flops | bytes accessed | tf_op | source)
XLA Modules:
  0.0 759.1 jit_solution(11054234781835128620)
XLA Ops:
  7.2 3.2 copy.29
  10.9 22.4 %reduce = bf16[4096,128]{1,0:T(8,128)(2,1)S(1)} reduce(bf16[4096,1,128]{2,1,0:T(2,128)(2,1)S(1)} %bitcast.55, bf16[]{:T(256)} %broadcast.7), dimensions={1}, to_apply=%bitcast.54.reduce_sub_computation | reduce | bytes 2097154
  33.3 1.1 reshape.24
  34.4 17.0 %all-to-all-start = ((bf16[32,2,8192]{2,1,0:T(2,128)(2,1)}), bf16[32,2,8192]{2,1,0:T(2,128)(2,1)S(1)}, u32[]{:S(2)}, u32[]{:S(2)}) async-start(bf16[32,2,8192]{2,1,0:T(2,128)(2,1)} %reshape.24), calls=%async_computation | async-start | bytes 2097152 | tf_op jit(solution)/shard_map/all_to_all | solution.py:34
  51.4 3.2 copy.28
  54.6 23.4 %reduce.1 = bf16[4096,128]{1,0:T(8,128)(2,1)} reduce(bf16[4096,1,128]{2,1,0:T(2,128)(2,1)S(1)} %bitcast.56, bf16[]{:T(256)} %broadcast.7), dimensions={1}, to_apply=%bitcast.53.reduce_sub_computation | reduce | bytes 2097154
  78.0 2.1 reshape.26
  80.1 21.0 %all-to-all-done = bf16[32,2,8192]{2,1,0:T(2,128)(2,1)S(1)} async-done(((bf16[32,2,8192]{2,1,0:T(2,128)(2,1)}), bf16[32,2,8192]{2,1,0:T(2,128)(2,1)S(1)}, u32[]{:S(2)}, u32[]{:S(2)}) %all-to-all-start) | async-done | bytes 1048608 | tf_op jit(solution)/shard_map/all_to_all | solution.py:34
  101.1 9.3 %all-to-all-start.1 = ((bf16[32,2,8192]{2,1,0:T(2,128)(2,1)}), bf16[32,2,8192]{2,1,0:T(2,128)(2,1)}, u32[]{:S(2)}, u32[]{:S(2)}) async-start(bf16[32,2,8192]{2,1,0:T(2,128)(2,1)} %reshape.26), calls=%async_computation.1 | async-start | bytes 2097152 | tf_op jit(solution)/shard_map/all_to_all | solution.py:35
  111.3 3.4 collective-permute-start
  114.8 14.6 %all_gather.10 = bf16[1152,128]{1,0:T(8,128)(2,1)S(1)} all-gather(bf16[144,128]{1,0:T(8,128)(2,1)S(1)} %copy-done.8), channel_id=1, replica_groups=mesh['sp'=32,'fsdp'=8,'dp'=2] {'fsdp'}, dimensions={0}, use_global_device_ids=true | all-gather | bytes 331776 | tf_op jit(solution)/shard_map/all_gather | solution.py:64
  129.7 18.6 %collective-permute-done = bf16[3,4096]{1,0:T(4,128)(2,1)S(1)} collective-permute-done((bf16[3,4096]{1,0:T(4,128)(2,1)S(1)}, bf16[3,4096]{1,0:T(4,128)(2,1)S(1)}, u32[]{:S(2)}, u32[]{:S(2)}) %collective-permute-start) | collective-permute-done | bytes 24608 | tf_op jit(solution)/shard_map/ppermute | solution.py:12
  148.3 1.5 maximum_convert_fusion
  149.8 5.8 reshape.25
  155.6 3.8 bitcast_convert_fusion
  159.4 1.2 copy.18
  160.6 2.4 fusion.8
  164.0 1.3 collective-permute-start.1
  165.3 5.8 reshape.27
  171.0 3.8 convert_negate_fusion
  174.8 2.5 copy.20
  177.4 3.5 convert_reduce_fusion
  180.9 1.9 fusion.22
  183.3 1.1 convolution_bitcast_fusion
  184.7 1.1 multiply_reduce_fusion.3
  187.5 116.6 %psum.31 = f32[4096]{0:T(1024)S(1)} all-reduce(f32[4096]{0:T(1024)S(1)} %get-tuple-element.26), channel_id=1, replica_groups=mesh['sp'=32,'fsdp'=8,'dp'=2] {'sp','fsdp','dp'}, use_global_device_ids=true, to_apply=%region_8.0 | all-reduce | flops 4096 | bytes 32768 | tf_op jit(solution)/shard_map/psum | solution.py:85
  304.7 376.1 %all-reduce.3.cloned.1.call-done = (f32[1152,128]{0,1:T(8,128)}, f32[128,4096]{1,0:T(8,128)}, f32[4,4096]{1,0:T(4,128)}) async-done(((f32[1152,128]{0,1:T(8,128)}, f32[128,4096]{1,0:T(8,128)}, f32[4,4096]{1,0:T(4,128)}), (f32[1152,128]{0,1:T(8,128)}, f32[128,4096]{1,0:T(8,128)}, f32[4,4096]{1,0:T(4,128)})) %all-reduce.3.cloned.1.call-update) | async-done | bytes 2752528 | tf_op jit(solution)/shard_map/psum | solution.py:85
  680.8 1.0 dynamic-slice_multiply_fusion
  682.5 1.3 dynamic-slice_multiply_fusion.1
  683.8 1.4 dynamic-slice_multiply_fusion.2
  685.3 59.4 %all-gather.3.cloned.1.call-done = bf16[1152,4096]{1,0:T(8,128)(2,1)} async-done(((bf16[144,4096]{1,0:T(8,128)(2,1)}), bf16[1152,4096]{1,0:T(8,128)(2,1)}) %all-gather.3.cloned.1.call-update) | async-done | bytes 9437200 | tf_op jit(solution)/shard_map/all_gather | solution.py:63
  744.6 6.9 fusion.13
  (40 shorter events, 7.5 us)
Async XLA Ops:
  7.2 122.3 %copy-start = (bf16[1,128,1152]{2,1,0:T(8,128)(2,1)S(1)}, bf16[1,128,1152]{2,1,0:T(8,128)(2,1)}, u32[]{:S(2)}) copy-start(bf16[1,128,1152]{2,1,0:T(8,128)(2,1)} %param.9) | copy-start | bytes 884740
  34.4 66.7 %all-to-all-start = ((bf16[32,2,8192]{2,1,0:T(2,128)(2,1)}), bf16[32,2,8192]{2,1,0:T(2,128)(2,1)S(1)}, u32[]{:S(2)}, u32[]{:S(2)}) async-start(bf16[32,2,8192]{2,1,0:T(2,128)(2,1)} %reshape.24), calls=%async_computation | async-start | bytes 2097152 | tf_op jit(solution)/shard_map/all_to_all | solution.py:34
  78.0 36.8 %copy-start.8 = (bf16[144,128]{1,0:T(8,128)(2,1)S(1)}, bf16[144,128]{1,0:T(8,128)(2,1)}, u32[]{:S(2)}) copy-start(bf16[144,128]{1,0:T(8,128)(2,1)} %param.14) | copy-start | bytes 110596
  78.0 51.4 %copy-start.7 = (bf16[4,4096]{1,0:T(4,128)(2,1)S(1)}, bf16[4,4096]{1,0:T(4,128)(2,1)}, u32[]{:S(2)}) copy-start(bf16[4,4096]{1,0:T(4,128)(2,1)} %param.17) | copy-start | bytes 98308
  101.1 47.2 %copy-start.5 = (bf16[32,2,8192]{2,1,0:T(2,128)(2,1)}, bf16[32,2,8192]{2,1,0:T(2,128)(2,1)S(1)}, u32[]{:S(2)}) copy-start(bf16[32,2,8192]{2,1,0:T(2,128)(2,1)S(1)} %all-to-all-done) | copy-start | bytes 3145732
  101.1 64.2 %all-to-all-start.1 = ((bf16[32,2,8192]{2,1,0:T(2,128)(2,1)}), bf16[32,2,8192]{2,1,0:T(2,128)(2,1)}, u32[]{:S(2)}, u32[]{:S(2)}) async-start(bf16[32,2,8192]{2,1,0:T(2,128)(2,1)} %reshape.26), calls=%async_computation.1 | async-start | bytes 2097152 | tf_op jit(solution)/shard_map/all_to_all | solution.py:35
  110.4 67.0 %all-gather.5.cloned.1.call-start = ((), (), s32[]{:S(2)}) async-start(), calls=%async_computation.3 | async-start | bytes 1179648 | tf_op jit(solution)/shard_map/all_gather | solution.py:65
  111.3 37.0 %collective-permute-start = (bf16[3,4096]{1,0:T(4,128)(2,1)S(1)}, bf16[3,4096]{1,0:T(4,128)(2,1)S(1)}, u32[]{:S(2)}, u32[]{:S(2)}) collective-permute-start(bf16[3,4096]{1,0:T(4,128)(2,1)S(1)} %slice_bitcast_fusion), channel_id=1, source_target_pairs={{0,16},{16,32},{32,48},{48,64},{64,80},{80,96},{96,112},{112,128},... | collective-permute-start | bytes 73736 | tf_op jit(solution)/shard_map/ppermute | solution.py:12
  114.8 566.0 %all-reduce.3.cloned.1.call-start = ((), (), s32[]{:S(2)}) async-start(), calls=%async_computation.4 | async-start | bytes 5505024 | tf_op jit(solution)/shard_map/psum | solution.py:85
  163.0 1.0 copy-start.3
  164.0 20.4 %collective-permute-start.1 = (bf16[3,4096]{1,0:T(4,128)(2,1)S(1)}, bf16[3,4096]{1,0:T(4,128)(2,1)S(1)}, u32[]{:S(2)}, u32[]{:S(2)}) collective-permute-start(bf16[3,4096]{1,0:T(4,128)(2,1)S(1)} %slice.80), channel_id=1, source_target_pairs={{16,0},{32,16},{48,32},{64,48},{80,64},{96,80},{112,96},{128,112},... | collective-permute-start | bytes 73736 | tf_op jit(solution)/shard_map/ppermute | solution.py:12
  174.8 2.6 copy-start.9
  180.9 1.9 copy-start.6
  182.8 1.6 copy-start.4
  184.6 1.3 copy-start.1
  186.7 558.0 %copy-start.2 = (f32[131,4096]{1,0:T(8,128)S(1)}, f32[131,4096]{1,0:T(8,128)}, u32[]{:S(2)}) copy-start(f32[131,4096]{1,0:T(8,128)} %copy-done.1) | copy-start | bytes 6438916
  186.7 557.9 %all-gather.3.cloned.1.call-start = ((), (), s32[]{:S(2)}) async-start(), calls=%async_computation.2 | async-start | bytes 10616832 | tf_op jit(solution)/shard_map/all_gather | solution.py:63
Sparse Core Ops, SparseCore 0:
  114.9 31.6 all-gather.4
  186.8 493.9 all-reduce.2
  682.9 61.6 all-gather.2
where the time goes:
time: 760 us; the launch traced here: 759 us
  waiting for transfers between devices  476 us (63%)
  blocking collectives  131 us (17%)
  other arithmetic  63.6 us (8%)
  starting transfers between devices  31.1 us (4%)
  local copies, waits for them, and re-layouts  28.4 us (4%)
  matrix products  15.1 us (2%)
  between operations  14 us (2%)
    psum x1, waiting for transfers between devices, per_device(): lax.psum((down_term, up_term, conv_term, bias_term), ('sp', 'fsdp', 'dp'))  376 us
    psum x1, blocking collectives, per_device(): lax.psum((down_term, up_term, conv_term, bias_term), ('sp', 'fsdp', 'dp'))  117 us
    all_gather x1, waiting for transfers between devices, per_device(): lax.all_gather(key_weight, 'fsdp', axis=0, tiled=True)  59.4 us
    unnamed x2, other arithmetic  45.8 us
    unnamed x28, local copies, waits for them, and re-layouts  23.7 us
    all_to_all x1, waiting for transfers between devices, per_device(): lax.all_to_all(key_cot, 'sp', split_axis=1, concat_axis=2, tiled=True)  21 us
    ppermute x2, waiting for transfers between devices, shifted(): return lax.ppermute(block, axis, route)  18.6 us
    all_to_all x1, starting transfers between devices, per_device(): lax.all_to_all(key_cot, 'sp', split_axis=1, concat_axis=2, tiled=True)  17 us
  transfers between devices with their start and end apart: 7, of which 4 were waited for; matrix products, arithmetic and copies ran while one was open for 9% of the time, Pallas kernels for 0%

commit v1 on v0

v1 whole, which is shorter than its diff:
```python
import functools

import jax
import jax.numpy as jnp
from jax import lax
from jax.experimental import pallas as pl
from jax.experimental.pallas import tpu as pltpu
from jax.sharding import Mesh
from jax.sharding import PartitionSpec as P

CONV = 4
BF16 = jnp.bfloat16
F32 = jnp.float32
LANES = 128
SP = ("xl", "zh", "zl")
PLANE = ("fsdp", "xl", "dp")
VMEM = 16 * 2**20
PADDED = 48


def key_kernel(
    cot_ref, key_ref, before_ref, taps_ref, tokens_ref, part0, part1, part2, part3, bias_ref, up_ref,
    slope_ref, send_ref, latent_ref, ext_ref, down_ref,
):
    step = pl.program_id(0)
    blocks, rows, _ = cot_ref.shape
    ups = up_ref.shape[1]

    @pl.when(step == 0)
    def _():
        latent_grad = sum(part[...].astype(F32) for part in (part0, part1, part2, part3)).astype(BF16)
        latent_ref[...] = latent_grad
        down_ref[...] = lax.dot_general(
            tokens_ref[...], latent_grad, (((0,), (0,)), ((), ())), preferred_element_type=F32
        )

    taps = taps_ref[...].astype(F32)
    ext_ref[:8, :] = before_ref[...].astype(F32)
    ext_ref[8:, :] = key_ref[...].astype(F32)
    share = down_ref.shape[0] // (blocks * pl.num_programs(0))
    own = blocks * share
    down = down_ref[pl.ds(pl.multiple_of(step * own, 8), own), :]
    for block in range(blocks):
        cols = slice(block * LANES, (block + 1) * LANES)
        shifted_keys = [ext_ref[8 - j : 8 - j + rows, cols] for j in range(CONV)]
        conv_out = sum(taps[j : j + 1, cols] * shifted_keys[j] for j in range(CONV))
        squashed = jax.nn.sigmoid(conv_out)
        slope = squashed * (1.0 + conv_out * (1.0 - squashed))
        grad = (cot_ref[block].astype(F32) * slope).astype(BF16)
        slope_ref[:, cols] = grad
        grad = grad.astype(F32)
        terms = [down[block * share : (block + 1) * share]]
        terms += [jnp.sum(grad * shifted_keys[j], axis=0, keepdims=True) for j in range(CONV)]
        terms += [bias_ref[block], jnp.zeros((PADDED - share - CONV - 1, LANES), F32)]
        send_ref[block, :ups, :] = up_ref[block]
        send_ref[block, ups:, :] = jnp.concatenate(terms, axis=0).astype(BF16)


def key_stage(cot, keys, before, taps, tokens, parts, bias, ups):
    heads, rows, _ = cot.shape
    step = 4
    wide = step * LANES
    ups_rows = ups.shape[1]
    whole = lambda array: pl.BlockSpec(array.shape, lambda i: (0, 0))
    return pl.pallas_call(
        key_kernel,
        grid=(heads // step,),
        in_specs=[
            pl.BlockSpec((step, rows, LANES), lambda i: (i, 0, 0)),
            pl.BlockSpec((rows, wide), lambda i: (0, i)),
            pl.BlockSpec((8, wide), lambda i: (0, i)),
            pl.BlockSpec((CONV, wide), lambda i: (0, i)),
            whole(tokens),
            *(whole(part) for part in parts),
            pl.BlockSpec((step, 1, LANES), lambda i: (i, 0, 0)),
            pl.BlockSpec((step, ups_rows, LANES), lambda i: (i, 0, 0)),
        ],
        out_specs=[
            pl.BlockSpec((rows, wide), lambda i: (0, i)),
            pl.BlockSpec((step, ups_rows + PADDED, LANES), lambda i: (i, 0, 0)),
            whole(parts[0]),
        ],
        out_shape=[
            jax.ShapeDtypeStruct((rows, heads * LANES), BF16),
            jax.ShapeDtypeStruct((heads, ups_rows + PADDED, LANES), BF16),
            jax.ShapeDtypeStruct(parts[0].shape, BF16),
        ],
        scratch_shapes=[
            pltpu.VMEM((rows + 8, wide), F32),
            pltpu.VMEM((tokens.shape[1], LANES), F32),
        ],
        compiler_params=pltpu.CompilerParams(vmem_limit_bytes=VMEM),
        cost_estimate=pl.CostEstimate(
            flops=40 * heads * rows * LANES, bytes_accessed=3 * 2**20, transcendentals=heads * rows * LANES
        ),
        name="key_stage",
    )(cot, keys, before, taps, tokens, *parts, bias, ups)


def gate_kernel(
    at_ref, cot_ref, lat_ref, up_ref, bias_ref,
    part0, part1, part2, part3, send_ref, bias_out, sum_ref, grad_ref,
):
    zh = at_ref[0]
    rows = part0.shape[0]
    latent = lat_ref[...]
    ups = []
    for head in range(8):
        up_head = jnp.concatenate([up_ref[f, head] for f in range(8)], axis=0)
        ups.append(up_head)
        logits = jnp.dot(latent, up_head, preferred_element_type=F32) + bias_ref[head : head + 1, :]
        grad = (-cot_ref[head].astype(F32) * jax.nn.sigmoid(logits)).astype(BF16)
        grad_ref[head] = grad
        bias_out[head : head + 1, :] = jnp.sum(grad.astype(F32), axis=0, keepdims=True)
    partial = None
    for head in range(8):
        term = lax.dot_general(
            grad_ref[head], ups[head], (((1,), (1,)), ((), ())), preferred_element_type=F32
        )
        partial = term if partial is None else partial + term
    sum_ref[...] = partial.astype(BF16)
    for k, part in enumerate((part0, part1, part2, part3)):
        owner = lax.rem(zh + k, 4)
        part[...] = sum_ref[pl.ds(pl.multiple_of(owner * rows, rows), rows), :]
    for x in range(2):
        terms = [
            lax.dot_general(
                latent, grad_ref[x * 4 + zl], (((0,), (0,)), ((), ())), preferred_element_type=F32
            )
            for zl in range(4)
        ]
        for f in range(8):
            for dp in range(2):
                first = (f * 2 + dp) * 8
                send_ref[f * 4 + x * 2 + dp] = jnp.concatenate(
                    [term[first : first + 8] for term in terms], axis=0
                ).astype(BF16)


def gate_stage(at, cot, lat, up_rows, bias):
    tall, rank = lat.shape
    rows = tall // 4
    whole = pl.BlockSpec(memory_space=pltpu.VMEM)
    part = jax.ShapeDtypeStruct((rows, rank), BF16)
    return pl.pallas_call(
        gate_kernel,
        in_specs=[pl.BlockSpec(memory_space=pltpu.SMEM)] + [whole] * 4,
        out_specs=[whole] * 6,
        out_shape=[part] * 4
        + [jax.ShapeDtypeStruct((32, 32, LANES), BF16), jax.ShapeDtypeStruct((8, LANES), F32)],
        scratch_shapes=[pltpu.VMEM((tall, rank), BF16), pltpu.VMEM((8, tall, LANES), BF16)],
        compiler_params=pltpu.CompilerParams(vmem_limit_bytes=VMEM),
        cost_estimate=pl.CostEstimate(
            flops=6 * 8 * tall * rank * LANES, bytes_accessed=3 * 2**20, transcendentals=8 * tall * LANES
        ),
        name="gate_stage",
    )(at, cot, lat, up_rows, bias)


def input_kernel(slope_ref, after_ref, taps_ref, key_ref, latent_ref, down_ref, out_ref, sum_ref, ext_ref):
    step = pl.program_id(0)
    rows = slope_ref.shape[0]
    contract = (((1,), (1,)), ((), ()))

    @pl.when(step == 0)
    def _():
        sum_ref[...] = lax.dot_general(
            latent_ref[...], down_ref[...], contract, preferred_element_type=F32
        )

    taps = taps_ref[...].astype(F32)
    ext_ref[:rows, :] = slope_ref[...].astype(F32)
    ext_ref[rows:, :] = after_ref[...].astype(F32)
    grad = sum(taps[j : j + 1, :] * ext_ref[j : j + rows, :] for j in range(CONV)).astype(BF16)
    sum_ref[...] += lax.dot_general(grad, key_ref[...], contract, preferred_element_type=F32)

    @pl.when(step == pl.num_programs(0) - 1)
    def _():
        out_ref[...] = sum_ref[...].astype(BF16)


def input_stage(slope, after, taps, key_full, latent_grad, down_full):
    rows, channels = slope.shape
    width = key_full.shape[0]
    wide = 512
    return pl.pallas_call(
        input_kernel,
        grid=(channels // wide,),
        in_specs=[
            pl.BlockSpec((rows, wide), lambda i: (0, i)),
            pl.BlockSpec((8, wide), lambda i: (0, i)),
            pl.BlockSpec((CONV, wide), lambda i: (0, i)),
            pl.BlockSpec((width, wide), lambda i: (0, i)),
            pl.BlockSpec(latent_grad.shape, lambda i: (0, 0)),
            pl.BlockSpec(down_full.shape, lambda i: (0, 0)),
        ],
        out_specs=pl.BlockSpec((rows, width), lambda i: (0, 0)),
        out_shape=jax.ShapeDtypeStruct((rows, width), BF16),
        scratch_shapes=[pltpu.VMEM((rows, width), F32), pltpu.VMEM((rows + 8, wide), F32)],
        compiler_params=pltpu.CompilerParams(vmem_limit_bytes=VMEM),
        cost_estimate=pl.CostEstimate(
            flops=20 * 2 * rows * channels * width, bytes_accessed=80 * 2**20, transcendentals=0
        ),
        name="input_stage",
    )(slope, after, taps, key_full, latent_grad, down_full)


def finish_kernel(at_ref, shares_ref, down_ref, up_ref, conv_ref, bias_ref):
    xl = at_ref[0]
    shares, own_up = shares_ref.shape[0], up_ref.shape[0] // 2
    share = down_ref.shape[0] // shares
    for k in range(2):
        up_ref[k * own_up : (k + 1) * own_up, :] = shares_ref[2 * xl + k, :own_up, :]
    for i in range(shares):
        last = own_up + share
        down_ref[i * share : (i + 1) * share, :] = shares_ref[i, own_up:last, :]
        conv_ref[:, i * LANES : (i + 1) * LANES] = shares_ref[i, last : last + CONV, :]
        bias_ref[i : i + 1, :] = shares_ref[i, last + CONV : last + CONV + 1, :]


def finish_stage(at, shares, rows_down, rows_up):
    whole = pl.BlockSpec(memory_space=pltpu.VMEM)
    return pl.pallas_call(
        finish_kernel,
        in_specs=[pl.BlockSpec(memory_space=pltpu.SMEM), whole],
        out_specs=[whole] * 4,
        out_shape=[
            jax.ShapeDtypeStruct((rows_down, LANES), F32),
            jax.ShapeDtypeStruct((rows_up, LANES), F32),
            jax.ShapeDtypeStruct((CONV, shares.shape[0] * LANES), F32),
            jax.ShapeDtypeStruct((shares.shape[0], LANES), F32),
        ],
        compiler_params=pltpu.CompilerParams(vmem_limit_bytes=VMEM),
        name="finish_stage",
    )(at, shares)


def turned(block, axis, distance, size=4):
    return lax.ppermute(block, axis, [(i, (i + distance) % size) for i in range(size)])


def per_device(
    tokens, key_proj, key_cot, gate_cot, key_weight, gate_down, gate_up, gate_bias, conv_weight
):
    length = tokens.shape[1]
    count = 32
    rank = gate_down.shape[1]
    rows_down, rows_up = gate_down.shape[0], gate_up.shape[0]
    inputs, projected = tokens[0], key_proj[0]
    zh = lax.axis_index("zh")

    gate_blocks = gate_cot.reshape(2, 4, 4, length, LANES).transpose(0, 2, 1, 3, 4)
    gate_mid = lax.all_to_all(
        gate_blocks.reshape(8, 4 * length, LANES), ("xl", "zl"), 0, 0, tiled=True
    )
    before = lax.ppermute(projected[length - 8 :], SP, [(i, i + 1) for i in range(count - 1)])
    key_full = lax.all_gather(key_weight, "fsdp", axis=0, tiled=True)

    up_mine = lax.dynamic_index_in_dim(gate_up.reshape(rows_up, 2, 4, 4, LANES), zh, 2, False)
    up_mine = up_mine.reshape(rows_up, 8, LANES).transpose(1, 0, 2).reshape(8 * rows_up, LANES)
    factors = lax.all_gather(
        jnp.concatenate([gate_down, up_mine], axis=0), "fsdp", axis=0, tiled=False
    )
    down_full = factors[:, :rows_down].reshape(8 * rows_down, rank)
    up_rows = factors[:, rows_down:].reshape(8, 8, rows_up, LANES)
    latent = jnp.dot(inputs, down_full, preferred_element_type=F32).astype(BF16)
    lat_all = lax.all_gather(latent, "zh", axis=0, tiled=True)
    bias_mine = lax.dynamic_index_in_dim(gate_bias.reshape(2, 4, 4, LANES), zh, 1, False)
    *parts, up_send, bias_term = gate_stage(
        zh.astype(jnp.int32).reshape(1), gate_mid, lat_all, up_rows, bias_mine.reshape(8, LANES)
    )
    parts, key_cot = lax.optimization_barrier((parts, key_cot))
    key_seq = lax.all_to_all(key_cot.reshape(count, length, LANES), SP, 0, 0, tiled=True)
    parts = parts[:1] + [turned(parts[k], "zh", k) for k in range(1, 4)]
    bias_row = lax.dynamic_update_slice_in_dim(
        jnp.zeros((2, 4, 4, LANES), F32), bias_term.reshape(2, 1, 4, LANES), zh, 1
    ).reshape(count, 1, LANES)
    slope_grad, send, latent_grad = key_stage(
        key_seq, projected, before, conv_weight, inputs, parts, bias_row, up_send
    )

    following = lax.ppermute(slope_grad[:8], SP, [(i + 1, i) for i in range(count - 1)])
    plane = jnp.sum(lax.all_to_all(send, PLANE, 0, 0, tiled=True).astype(F32), axis=0)
    rows_share, own_up = rows_down // 4, rows_up // 2
    mixed = rows_share + CONV + 1
    same = (jnp.arange(4) == zh).reshape(4, 1, 1, 1)
    to_heads = jnp.where(same, plane[: 4 * own_up].reshape(1, 4, own_up, LANES), 0.0)
    to_all = jnp.broadcast_to(plane[4 * own_up : 4 * own_up + mixed], (4, 4, mixed, LANES))
    line = jnp.concatenate([to_heads, to_all], axis=2).astype(BF16)
    line = lax.all_to_all(
        line.reshape(16, own_up + mixed, LANES), ("zh", "zl"), 0, 0, tiled=True
    )
    input_grad = input_stage(
        slope_grad, following, conv_weight, key_full, latent_grad, down_full
    )[None]
    line, input_grad = lax.optimization_barrier((line, input_grad))
    done = jnp.sum(line.astype(F32), axis=0) * float(65536) ** (-0.5)
    shares = lax.all_to_all(
        jnp.broadcast_to(done[None], (4,) + done.shape), ("xl", "dp"), 0, 0, tiled=True
    )

    at = lax.axis_index("xl").astype(jnp.int32).reshape(1)
    down_own, up_own, conv_own, bias_own = finish_stage(at, shares, rows_down, rows_up)
    return input_grad, down_own, up_own, conv_own, bias_own.reshape(4 * LANES)


def solution(mesh):
    fine = Mesh(mesh.devices.reshape(2, 4, 4, 8, 2), ("xl", "zh", "zl", "fsdp", "dp"))
    windows = ("fsdp", "dp")
    return jax.shard_map(
        per_device,
        mesh=fine,
        in_specs=(
            P(windows, SP, None),
            P(windows, SP, None),
            P(windows, None, SP),
            P(windows, None, SP),
            P("fsdp", None),
            P("fsdp", None),
            P("fsdp", None),
            P(),
            P(),
        ),
        out_specs=(
            P(windows, SP, None),
            P("fsdp", None),
            P("fsdp", SP),
            P(None, "fsdp"),
            P("fsdp"),
        ),
        check_vma=False,
    )
```

time: 760 us -> 195 us (0.26)
  waiting for transfers between devices: 476 us -> 55.7 us
  blocking collectives: 131 us -> 35 us
  other arithmetic: 63.6 us -> 0.96 us
  starting transfers between devices: 31.1 us -> 66.2 us
  local copies, waits for them, and re-layouts: 28.4 us -> 7.26 us
  matrix products: 15.1 us -> 0.23 us
  Pallas kernels: 0 us -> 12.8 us
    psum x1 -> x0, waiting for transfers between devices: 376 us -> none  [per_device(): lax.psum((down_term, up_term, conv_term, bias_term), ('sp', 'fsdp', 'dp'))]
    psum x1 -> x0, blocking collectives: 117 us -> none  [per_device(): lax.psum((down_term, up_term, conv_term, bias_term), ('sp', 'fsdp', 'dp'))]
    all_gather x2 -> x1, waiting for transfers between devices: 59.4 us -> 0.02 us  [per_device(): key_full = lax.all_gather(key_weight, 'fsdp', axis=0, tiled=True)]
    unnamed x2 -> x0, other arithmetic: 45.8 us -> none
    all_gather x1 -> x2, blocking collectives: 14.6 us -> 35 us  [the longest x1 19 us: per_device(): lat_all = lax.all_gather(latent, 'zh', axis=0, tiled=True)]
    ppermute x2 -> x5, starting transfers between devices: 4.69 us -> 24.5 us  [the longest x3 20.1 us: turned(): lax.ppermute(block, axis, [(i, (i + distance) % size) for i in range(size)])]
    ppermute x2 -> x5, waiting for transfers between devices: 18.6 us -> 37.8 us  [the longest x3 26.9 us: turned(): lax.ppermute(block, axis, [(i, (i + distance) % size) for i in range(size)])]
    unnamed x28 -> x20, local copies, waits for them, and re-layouts: 23.7 us -> 5.19 us
  transfers between devices with their start and end apart: 7 -> 11, of which waited for: 4 -> 6; matrix products, arithmetic and copies ran while one was open for 9% -> 1% of each run, Pallas kernels for 0% -> 6%
where the time goes in v1:
time: 195 us; the launch traced here: 193 us
  starting transfers between devices  66.2 us (34%)
  waiting for transfers between devices  55.7 us (29%)
  blocking collectives  35 us (18%)
  between operations  14.3 us (7%)
  Pallas kernels  12.8 us (7%)
  local copies, waits for them, and re-layouts  7.26 us (4%)
    ppermute x3, waiting for transfers between devices, turned(): lax.ppermute(block, axis, [(i, (i + distance) % size) for i in range(size)])  26.9 us
    ppermute x3, starting transfers between devices, turned(): lax.ppermute(block, axis, [(i, (i + distance) % size) for i in range(size)])  20.1 us
    all_gather x1, blocking collectives, per_device(): lat_all = lax.all_gather(latent, 'zh', axis=0, tiled=True)  19 us
    all_gather x1, blocking collectives, per_device(): lax.all_gather(jnp.concatenate([gate_down, up_mine], axis=0), 'fsdp', axi...  16.1 us
    all_to_all x1, starting transfers between devices, per_device(): lax.all_to_all(key_cot.reshape(count, length, LANES), SP, 0, 0, tiled=True)  13.8 us
    ppermute x1, waiting for transfers between devices, per_device(): lax.ppermute(projected[length - 8:], SP, [(i, i + 1) for i in range(count...  10.9 us
    all_to_all x1, waiting for transfers between devices, per_device(): lax.all_to_all(send, PLANE, 0, 0, tiled=True).astype(F32)  10 us
    all_to_all x1, starting transfers between devices, per_device(): lax.all_to_all(send, PLANE, 0, 0, tiled=True).astype(F32)  9.31 us
  transfers between devices with their start and end apart: 11, of which 6 were waited for; matrix products, arithmetic and copies ran while one was open for 1% of the time, Pallas kernels for 6%

profile of v1, /device:TPU:1, one launch (start us, length us, event | category | flops | bytes accessed | tf_op | source)
XLA Modules:
  0.0 192.5 jit_solution(3427625837738216829)
XLA Ops:
  7.2 0.7 all-gather.3.cloned.1.call-update
  7.9 0.5 copy-done.7
  8.4 1.1 copy.29
  9.5 7.5 %all-to-all-start = ((bf16[8,512,128]{2,1,0:T(8,128)(2,1)}), bf16[8,512,128]{2,1,0:T(8,128)(2,1)S(1)}, u32[]{:S(2)}, u32[]{:S(2)}) async-start(bf16[8,512,128]{2,1,0:T(8,128)(2,1)} %bitcast.3), calls=%async_computation | async-start | bytes 2097152 | tf_op jit(solution)/shard_map/all_to_all | solution.py:253
  17.2 16.1 %all-gather = bf16[2176,128]{1,0:T(8,128)(2,1)S(1)} all-gather(bf16[272,128]{1,0:T(8,128)(2,1)S(1)} %pad_maximum_fusion.1), channel_id=2, replica_groups=mesh['xl'=2,'zh'=4,'zl'=4,'fsdp'=8,'dp'=2] {'fsdp'}, dimensions={0}, use_global_device_ids=true | all-gather | bytes 626688 | tf_op jit(solution)/shard_map/all_gather | solution.py:261
  33.3 0.2 fusion
  33.5 19.0 %all_gather.14.lat_ref = bf16[512,128]{1,0:T(8,128)(2,1)S(1)} all-gather(bf16[128,128]{1,0:T(8,128)(2,1)S(1)} %fusion), channel_id=1, replica_groups=mesh['xl'=2,'zh'=4,'zl'=4,'fsdp'=8,'dp'=2] {'zh'}, dimensions={0}, use_global_device_ids=true | all-gather | bytes 163840 | tf_op jit(solution)/shard_map/all_gather | solution.py:267
  52.5 1.1 gate_stage.1
  53.7 13.8 %all-to-all-start.1 = ((bf16[32,128,128]{2,1,0:T(8,128)(2,1)}), bf16[32,128,128]{2,1,0:T(8,128)(2,1)S(1)}, u32[]{:S(2)}, u32[]{:S(2)}) async-start(bf16[32,128,128]{2,1,0:T(8,128)(2,1)} %bitcast.50), calls=%async_computation.1 | async-start | bytes 2097152 | tf_op jit(solution)/shard_map/all_to_all | solution.py:273
  67.5 3.1 %collective-permute-start = (bf16[8,4096]{1,0:T(8,128)(2,1)S(1)}, bf16[8,4096]{1,0:T(8,128)(2,1)S(1)}, u32[]{:S(2)}, u32[]{:S(2)}) collective-permute-start(bf16[8,4096]{1,0:T(8,128)(2,1)S(1)} %slice_bitcast_fusion), channel_id=1, source_target_pairs={{0,16},{16,32},{32,48},{48,64},{64,80},{80,96},{96,112},{112,128},... | collective-permute-start | bytes 196616 | tf_op jit(solution)/shard_map/ppermute | solution.py:256
  70.6 7.0 %collective-permute-start.1 = (bf16[128,128]{1,0:T(8,128)(2,1)S(1)}, bf16[128,128]{1,0:T(8,128)(2,1)S(1)}, u32[]{:S(2)}, u32[]{:S(2)}) collective-permute-start(bf16[128,128]{1,0:T(8,128)(2,1)S(1)} %get-tuple-element.31), channel_id=1, source_target_pairs={{0,64},{64,128},{128,192},{192,0},{1,65},{65,129},{129,193},{193,1... | collective-permute-start | bytes 98312 | tf_op jit(solution)/shard_map/ppermute | solution.py:239
  77.6 6.1 %collective-permute-start.2 = (bf16[128,128]{1,0:T(8,128)(2,1)S(1)}, bf16[128,128]{1,0:T(8,128)(2,1)S(1)}, u32[]{:S(2)}, u32[]{:S(2)}) collective-permute-start(bf16[128,128]{1,0:T(8,128)(2,1)S(1)} %get-tuple-element.32), channel_id=1, source_target_pairs={{0,128},{64,192},{128,0},{192,64},{1,129},{65,193},{129,1},{193,65... | collective-permute-start | bytes 98312 | tf_op jit(solution)/shard_map/ppermute | solution.py:239
  83.7 7.0 %collective-permute-start.3 = (bf16[128,128]{1,0:T(8,128)(2,1)S(1)}, bf16[128,128]{1,0:T(8,128)(2,1)S(1)}, u32[]{:S(2)}, u32[]{:S(2)}) collective-permute-start(bf16[128,128]{1,0:T(8,128)(2,1)S(1)} %get-tuple-element.33), channel_id=1, source_target_pairs={{0,192},{64,0},{128,64},{192,128},{1,193},{65,1},{129,65},{193,129... | collective-permute-start | bytes 98312 | tf_op jit(solution)/shard_map/ppermute | solution.py:239
  90.8 10.9 %collective-permute-done.before_ref = bf16[8,4096]{1,0:T(8,128)(2,1)S(1)} collective-permute-done((bf16[8,4096]{1,0:T(8,128)(2,1)S(1)}, bf16[8,4096]{1,0:T(8,128)(2,1)S(1)}, u32[]{:S(2)}, u32[]{:S(2)}) %collective-permute-start) | collective-permute-done | bytes 65568 | tf_op jit(solution)/shard_map/ppermute | solution.py:256
  101.7 12.3 %collective-permute-done.1.part1 = bf16[128,128]{1,0:T(8,128)(2,1)S(1)} collective-permute-done((bf16[128,128]{1,0:T(8,128)(2,1)S(1)}, bf16[128,128]{1,0:T(8,128)(2,1)S(1)}, u32[]{:S(2)}, u32[]{:S(2)}) %collective-permute-start.1) | collective-permute-done | bytes 32800 | tf_op jit(solution)/shard_map/ppermute | solution.py:239
  113.9 14.6 %collective-permute-done.2.part2 = bf16[128,128]{1,0:T(8,128)(2,1)S(1)} collective-permute-done((bf16[128,128]{1,0:T(8,128)(2,1)S(1)}, bf16[128,128]{1,0:T(8,128)(2,1)S(1)}, u32[]{:S(2)}, u32[]{:S(2)}) %collective-permute-start.2) | collective-permute-done | bytes 32800 | tf_op jit(solution)/shard_map/ppermute | solution.py:239
  128.6 4.9 %key_stage.1 = (bf16[128,4096]{1,0:T(8,128)(2,1)S(1)}, bf16[32,80,128]{2,1,0:T(8,128)(2,1)}, bf16[128,128]{1,0:T(8,128)(2,1)S(1)}) custom-call(bf16[32,128,128]{2,1,0:T(8,128)(2,1)S(1)} %all-to-all-done.1.cot_ref, bf16[128,4096]{1,0:T(8,128)(2,1)S(1)} %bitcast.39, bf16[8,4096]{1,0:T(8,128)(2,1)S(1)} %collective-permute-done.before_ref, ...), custom_call_target="tpu_custom_call" | custom-call | flops 20971520 | bytes 3145728 | tf_op jit(solution)/shard_map/key_stage/pallas_call | solution.py:65
  133.4 1.0 copy-done.4
  134.4 9.3 %all-to-all-start.2 = ((bf16[32,80,128]{2,1,0:T(8,128)(2,1)}), bf16[32,80,128]{2,1,0:T(8,128)(2,1)S(1)}, u32[]{:S(2)}, u32[]{:S(2)}) async-start(bf16[32,80,128]{2,1,0:T(8,128)(2,1)} %get-tuple-element.36), calls=%async_computation.2 | async-start | bytes 1310720 | tf_op jit(solution)/shard_map/all_to_all | solution.py:283
  143.8 0.1 broadcast_in_dim.44
  143.9 1.3 collective-permute-start.4
  145.2 10.0 %all-to-all-done.2 = bf16[32,80,128]{2,1,0:T(8,128)(2,1)S(1)} async-done(((bf16[32,80,128]{2,1,0:T(8,128)(2,1)}), bf16[32,80,128]{2,1,0:T(8,128)(2,1)S(1)}, u32[]{:S(2)}, u32[]{:S(2)}) %all-to-all-start.2) | async-done | bytes 655392 | tf_op jit(solution)/shard_map/all_to_all | solution.py:283
  155.2 0.1 convert_reduce_fusion
  155.5 0.7 pad_maximum_fusion
  156.2 3.5 %all-to-all-start.3 = ((bf16[16,49,128]{2,1,0:T(8,128)(2,1)}), bf16[16,49,128]{2,1,0:T(8,128)(2,1)S(1)}, u32[]{:S(2)}, u32[]{:S(2)}) async-start(bf16[16,49,128]{2,1,0:T(8,128)(2,1)} %pad_maximum_fusion), calls=%async_computation.3 | async-start | bytes 458752 | tf_op jit(solution)/shard_map/all_to_all | solution.py:290
  159.8 3.7 %copy-done.6 = bf16[1152,4096]{1,0:T(8,128)(2,1)S(1)} copy-done((bf16[1152,4096]{1,0:T(8,128)(2,1)S(1)}, bf16[1152,4096]{1,0:T(8,128)(2,1)}, u32[]{:S(2)}) %copy-start.6) | copy-done | bytes 9437208
  163.5 6.1 %input_stage.1 = bf16[128,1152]{1,0:T(8,128)(2,1)} custom-call(bf16[128,4096]{1,0:T(8,128)(2,1)S(1)} %copy-done.5, bf16[8,4096]{1,0:T(8,128)(2,1)S(1)} %collective-permute-done.4.after_ref, bf16[4,4096]{1,0:T(4,128)(2,1)S(1)} %copy-done.3, bf16[1152,4096]{1,0:T(8,128)(2,1)S(1)} %copy-done.6, bf16[128,128]{1,0:T(8,128)(2,1)S(1)} %get-tuple-element.38.latent_ref, ...), custom_call_target="tpu_custom_call" | custom-call | flops 24159191040 | bytes 83886080 | tf_op jit(solution)/shard_map/input_stage/pallas_call | solution.py:186
  169.6 2.8 %all-to-all-done.3 = bf16[16,49,128]{2,1,0:T(8,128)(2,1)S(1)} async-done(((bf16[16,49,128]{2,1,0:T(8,128)(2,1)}), bf16[16,49,128]{2,1,0:T(8,128)(2,1)S(1)}, u32[]{:S(2)}, u32[]{:S(2)}) %all-to-all-start.3) | async-done | bytes 200736 | tf_op jit(solution)/shard_map/all_to_all | solution.py:290
  172.4 0.6 broadcast_in_dim.53
  173.0 7.6 %all-to-all-start.4 = ((f32[4,49,128]{2,1,0:T(8,128)}), f32[4,49,128]{2,1,0:T(8,128)S(1)}, u32[]{:S(2)}, u32[]{:S(2)}) async-start(f32[4,49,128]{2,1,0:T(8,128)} %broadcast_in_dim.53), calls=%async_computation.4 | async-start | bytes 229376 | tf_op jit(solution)/shard_map/all_to_all | solution.py:298
  180.6 4.4 %all-to-all-done.4.shares_ref = f32[4,49,128]{2,1,0:T(8,128)S(1)} async-done(((f32[4,49,128]{2,1,0:T(8,128)}), f32[4,49,128]{2,1,0:T(8,128)S(1)}, u32[]{:S(2)}, u32[]{:S(2)}) %all-to-all-start.4) | async-done | bytes 100384 | tf_op jit(solution)/shard_map/all_to_all | solution.py:298
  185.0 0.6 finish_stage.1
  (42 shorter events, 0.5 us)
Async XLA Ops:
  7.2 45.3 %copy-start = (f32[4096]{0:T(1024)S(1)}, f32[4096]{0:T(1024)}, u32[]{:S(2)}) copy-start(f32[4096]{0:T(1024)} %param.16) | copy-start | bytes 49156
  7.2 1.2 copy-start.7
  7.2 152.6 %all-gather.3.cloned.1.call-start = ((), (), s32[]{:S(2)}) async-start(), calls=%async_computation.5 | async-start | bytes 10616832 | tf_op jit(solution)/shard_map/all_gather | solution.py:257
  9.5 7.5 %copy-start.8 = (bf16[16,4096]{1,0:T(8,128)(2,1)S(1)}, bf16[16,4096]{1,0:T(8,128)(2,1)}, u32[]{:S(2)}) copy-start(bf16[16,4096]{1,0:T(8,128)(2,1)} %param.15) | copy-start | bytes 393220
  9.5 7.7 %copy-start.9 = (bf16[144,128]{1,0:T(8,128)(2,1)S(1)}, bf16[144,128]{1,0:T(8,128)(2,1)}, u32[]{:S(2)}) copy-start(bf16[144,128]{1,0:T(8,128)(2,1)} %param.14) | copy-start | bytes 110596
  9.5 43.0 %all-to-all-start = ((bf16[8,512,128]{2,1,0:T(8,128)(2,1)}), bf16[8,512,128]{2,1,0:T(8,128)(2,1)S(1)}, u32[]{:S(2)}, u32[]{:S(2)}) async-start(bf16[8,512,128]{2,1,0:T(8,128)(2,1)} %bitcast.3), calls=%async_computation | async-start | bytes 2097152 | tf_op jit(solution)/shard_map/all_to_all | solution.py:253
  17.0 16.3 %copy-start.2 = (bf16[1,128,1152]{2,1,0:T(8,128)(2,1)S(1)}, bf16[1,128,1152]{2,1,0:T(8,128)(2,1)}, u32[]{:S(2)}) copy-start(bf16[1,128,1152]{2,1,0:T(8,128)(2,1)} %param.9) | copy-start | bytes 884740
  53.6 13.8 %copy-start.1 = (bf16[1,128,4096]{2,1,0:T(8,128)(2,1)S(1)}, bf16[1,128,4096]{2,1,0:T(8,128)(2,1)}, u32[]{:S(2)}) copy-start(bf16[1,128,4096]{2,1,0:T(8,128)(2,1)} %param.10) | copy-start | bytes 3145732
  53.6 74.9 %copy-start.3 = (bf16[4,4096]{1,0:T(4,128)(2,1)S(1)}, bf16[4,4096]{1,0:T(4,128)(2,1)}, u32[]{:S(2)}) copy-start(bf16[4,4096]{1,0:T(4,128)(2,1)} %taps_ref.3) | copy-start | bytes 98308
  53.7 74.9 %all-to-all-start.1 = ((bf16[32,128,128]{2,1,0:T(8,128)(2,1)}), bf16[32,128,128]{2,1,0:T(8,128)(2,1)S(1)}, u32[]{:S(2)}, u32[]{:S(2)}) async-start(bf16[32,128,128]{2,1,0:T(8,128)(2,1)} %bitcast.50), calls=%async_computation.1 | async-start | bytes 2097152 | tf_op jit(solution)/shard_map/all_to_all | solution.py:273
  67.5 34.2 %collective-permute-start = (bf16[8,4096]{1,0:T(8,128)(2,1)S(1)}, bf16[8,4096]{1,0:T(8,128)(2,1)S(1)}, u32[]{:S(2)}, u32[]{:S(2)}) collective-permute-start(bf16[8,4096]{1,0:T(8,128)(2,1)S(1)} %slice_bitcast_fusion), channel_id=1, source_target_pairs={{0,16},{16,32},{32,48},{48,64},{64,80},{80,96},{96,112},{112,128},... | collective-permute-start | bytes 196616 | tf_op jit(solution)/shard_map/ppermute | solution.py:256
  70.6 43.3 %collective-permute-start.1 = (bf16[128,128]{1,0:T(8,128)(2,1)S(1)}, bf16[128,128]{1,0:T(8,128)(2,1)S(1)}, u32[]{:S(2)}, u32[]{:S(2)}) collective-permute-start(bf16[128,128]{1,0:T(8,128)(2,1)S(1)} %get-tuple-element.31), channel_id=1, source_target_pairs={{0,64},{64,128},{128,192},{192,0},{1,65},{65,129},{129,193},{193,1... | collective-permute-start | bytes 98312 | tf_op jit(solution)/shard_map/ppermute | solution.py:239
  77.6 51.0 %collective-permute-start.2 = (bf16[128,128]{1,0:T(8,128)(2,1)S(1)}, bf16[128,128]{1,0:T(8,128)(2,1)S(1)}, u32[]{:S(2)}, u32[]{:S(2)}) collective-permute-start(bf16[128,128]{1,0:T(8,128)(2,1)S(1)} %get-tuple-element.32), channel_id=1, source_target_pairs={{0,128},{64,192},{128,0},{192,64},{1,129},{65,193},{129,1},{193,65... | collective-permute-start | bytes 98312 | tf_op jit(solution)/shard_map/ppermute | solution.py:239
  83.7 44.9 %collective-permute-start.3 = (bf16[128,128]{1,0:T(8,128)(2,1)S(1)}, bf16[128,128]{1,0:T(8,128)(2,1)S(1)}, u32[]{:S(2)}, u32[]{:S(2)}) collective-permute-start(bf16[128,128]{1,0:T(8,128)(2,1)S(1)} %get-tuple-element.33), channel_id=1, source_target_pairs={{0,192},{64,0},{128,64},{192,128},{1,193},{65,1},{129,65},{193,129... | collective-permute-start | bytes 98312 | tf_op jit(solution)/shard_map/ppermute | solution.py:239
  133.4 1.0 copy-start.4
  134.4 9.5 %copy-start.5 = (bf16[128,4096]{1,0:T(8,128)(2,1)S(1)}, bf16[128,4096]{1,0:T(8,128)(2,1)}, u32[]{:S(2)}) copy-start(bf16[128,4096]{1,0:T(8,128)(2,1)} %copy-done.4) | copy-start | bytes 3145732
  134.4 20.8 %all-to-all-start.2 = ((bf16[32,80,128]{2,1,0:T(8,128)(2,1)}), bf16[32,80,128]{2,1,0:T(8,128)(2,1)S(1)}, u32[]{:S(2)}, u32[]{:S(2)}) async-start(bf16[32,80,128]{2,1,0:T(8,128)(2,1)} %get-tuple-element.36), calls=%async_computation.2 | async-start | bytes 1310720 | tf_op jit(solution)/shard_map/all_to_all | solution.py:283
  143.9 15.8 %collective-permute-start.4 = (bf16[8,4096]{1,0:T(8,128)(2,1)S(1)}, bf16[8,4096]{1,0:T(8,128)(2,1)S(1)}, u32[]{:S(2)}, u32[]{:S(2)}) collective-permute-start(bf16[8,4096]{1,0:T(8,128)(2,1)S(1)} %slice.27), channel_id=1, source_target_pairs={{16,0},{32,16},{48,32},{64,48},{80,64},{96,80},{112,96},{128,112},... | collective-permute-start | bytes 196616 | tf_op jit(solution)/shard_map/ppermute | solution.py:282
  156.2 16.1 %all-to-all-start.3 = ((bf16[16,49,128]{2,1,0:T(8,128)(2,1)}), bf16[16,49,128]{2,1,0:T(8,128)(2,1)S(1)}, u32[]{:S(2)}, u32[]{:S(2)}) async-start(bf16[16,49,128]{2,1,0:T(8,128)(2,1)} %pad_maximum_fusion), calls=%async_computation.3 | async-start | bytes 458752 | tf_op jit(solution)/shard_map/all_to_all | solution.py:290
  159.8 3.7 %copy-start.6 = (bf16[1152,4096]{1,0:T(8,128)(2,1)S(1)}, bf16[1152,4096]{1,0:T(8,128)(2,1)}, u32[]{:S(2)}) copy-start(bf16[1152,4096]{1,0:T(8,128)(2,1)} %all-gather.3.cloned.1.call-done.key_ref) | copy-start | bytes 28311556
  173.0 12.0 %all-to-all-start.4 = ((f32[4,49,128]{2,1,0:T(8,128)}), f32[4,49,128]{2,1,0:T(8,128)S(1)}, u32[]{:S(2)}, u32[]{:S(2)}) async-start(f32[4,49,128]{2,1,0:T(8,128)} %broadcast_in_dim.53), calls=%async_computation.4 | async-start | bytes 229376 | tf_op jit(solution)/shard_map/all_to_all | solution.py:298
Sparse Core Ops, SparseCore 0:
  10.1 67.5 all-gather.2

commit v2 on v1

--- a/solution.py
+++ b/solution.py
@@ -18,28 +18,11 @@
 PADDED = 48
 
 
-def key_kernel(
-    cot_ref, key_ref, before_ref, taps_ref, tokens_ref, part0, part1, part2, part3, bias_ref, up_ref,
-    slope_ref, send_ref, latent_ref, ext_ref, down_ref,
-):
-    step = pl.program_id(0)
+def key_kernel(cot_ref, key_ref, before_ref, taps_ref, slope_ref, conv_ref, ext_ref):
     blocks, rows, _ = cot_ref.shape
-    ups = up_ref.shape[1]
-
-    @pl.when(step == 0)
-    def _():
-        latent_grad = sum(part[...].astype(F32) for part in (part0, part1, part2, part3)).astype(BF16)
-        latent_ref[...] = latent_grad
-        down_ref[...] = lax.dot_general(
-            tokens_ref[...], latent_grad, (((0,), (0,)), ((), ())), preferred_element_type=F32
-        )
-
     taps = taps_ref[...].astype(F32)
     ext_ref[:8, :] = before_ref[...].astype(F32)
     ext_ref[8:, :] = key_ref[...].astype(F32)
-    share = down_ref.shape[0] // (blocks * pl.num_programs(0))
-    own = blocks * share
-    down = down_ref[pl.ds(pl.multiple_of(step * own, 8), own), :]
     for block in range(blocks):
         cols = slice(block * LANES, (block + 1) * LANES)
         shifted_keys = [ext_ref[8 - j : 8 - j + rows, cols] for j in range(CONV)]
@@ -49,19 +32,15 @@
         grad = (cot_ref[block].astype(F32) * slope).astype(BF16)
         slope_ref[:, cols] = grad
         grad = grad.astype(F32)
-        terms = [down[block * share : (block + 1) * share]]
-        terms += [jnp.sum(grad * shifted_keys[j], axis=0, keepdims=True) for j in range(CONV)]
-        terms += [bias_ref[block], jnp.zeros((PADDED - share - CONV - 1, LANES), F32)]
-        send_ref[block, :ups, :] = up_ref[block]
-        send_ref[block, ups:, :] = jnp.concatenate(terms, axis=0).astype(BF16)
-
-
-def key_stage(cot, keys, before, taps, tokens, parts, bias, ups):
+        conv_ref[block] = jnp.concatenate(
+            [jnp.sum(grad * shifted_keys[j], axis=0, keepdims=True) for j in range(CONV)], axis=0
+        )
+
+
+def key_stage(cot, keys, before, taps):
     heads, rows, _ = cot.shape
     step = 4
     wide = step * LANES
-    ups_rows = ups.shape[1]
-    whole = lambda array: pl.BlockSpec(array.shape, lambda i: (0, 0))
     return pl.pallas_call(
         key_kernel,
         grid=(heads // step,),
@@ -70,31 +49,55 @@
             pl.BlockSpec((rows, wide), lambda i: (0, i)),
             pl.BlockSpec((8, wide), lambda i: (0, i)),
             pl.BlockSpec((CONV, wide), lambda i: (0, i)),
-            whole(tokens),
-            *(whole(part) for part in parts),
-            pl.BlockSpec((step, 1, LANES), lambda i: (i, 0, 0)),
-            pl.BlockSpec((step, ups_rows, LANES), lambda i: (i, 0, 0)),
         ],
         out_specs=[
             pl.BlockSpec((rows, wide), lambda i: (0, i)),
-            pl.BlockSpec((step, ups_rows + PADDED, LANES), lambda i: (i, 0, 0)),
-            whole(parts[0]),
+            pl.BlockSpec((step, CONV, LANES), lambda i: (i, 0, 0)),
         ],
         out_shape=[
             jax.ShapeDtypeStruct((rows, heads * LANES), BF16),
-            jax.ShapeDtypeStruct((heads, ups_rows + PADDED, LANES), BF16),
-            jax.ShapeDtypeStruct(parts[0].shape, BF16),
-        ],
-        scratch_shapes=[
-            pltpu.VMEM((rows + 8, wide), F32),
-            pltpu.VMEM((tokens.shape[1], LANES), F32),
-        ],
+            jax.ShapeDtypeStruct((heads, CONV, LANES), F32),
+        ],
+        scratch_shapes=[pltpu.VMEM((rows + 8, wide), F32)],
         compiler_params=pltpu.CompilerParams(vmem_limit_bytes=VMEM),
         cost_estimate=pl.CostEstimate(
             flops=40 * heads * rows * LANES, bytes_accessed=3 * 2**20, transcendentals=heads * rows * LANES
         ),
         name="key_stage",
-    )(cot, keys, before, taps, tokens, *parts, bias, ups)
+    )(cot, keys, before, taps)
+
+
+def pack_kernel(
+    tokens_ref, part0, part1, part2, part3, conv_ref, bias_ref, up_ref, send_ref, latent_ref
+):
+    latent_grad = sum(part[...].astype(F32) for part in (part0, part1, part2, part3)).astype(BF16)
+    latent_ref[...] = latent_grad
+    down = lax.dot_general(
+        tokens_ref[...], latent_grad, (((0,), (0,)), ((), ())), preferred_element_type=F32
+    )
+    peers, ups = up_ref.shape[0], up_ref.shape[1]
+    share = down.shape[0] // peers
+    rest = jnp.zeros((PADDED - share - CONV - 1, LANES), F32)
+    for peer in range(peers):
+        terms = [down[peer * share : (peer + 1) * share], conv_ref[peer], bias_ref[peer], rest]
+        send_ref[peer, :ups, :] = up_ref[peer]
+        send_ref[peer, ups:, :] = jnp.concatenate(terms, axis=0).astype(BF16)
+
+
+def pack_stage(tokens, parts, conv, bias, ups):
+    whole = pl.BlockSpec(memory_space=pltpu.VMEM)
+    peers, ups_rows, _ = ups.shape
+    return pl.pallas_call(
+        pack_kernel,
+        in_specs=[whole] * 8,
+        out_specs=[whole] * 2,
+        out_shape=[
+            jax.ShapeDtypeStruct((peers, ups_rows + PADDED, LANES), BF16),
+            jax.ShapeDtypeStruct(parts[0].shape, BF16),
+        ],
+        compiler_params=pltpu.CompilerParams(vmem_limit_bytes=VMEM),
+        name="pack_stage",
+    )(tokens, *parts, conv, bias, ups)
 
 
 def gate_kernel(
@@ -275,9 +278,9 @@
     bias_row = lax.dynamic_update_slice_in_dim(
         jnp.zeros((2, 4, 4, LANES), F32), bias_term.reshape(2, 1, 4, LANES), zh, 1
     ).reshape(count, 1, LANES)
-    slope_grad, send, latent_grad = key_stage(
-        key_seq, projected, before, conv_weight, inputs, parts, bias_row, up_send
-    )
+    slope_grad, conv_term = key_stage(key_seq, projected, before, conv_weight)
+    parts, conv_term = lax.optimization_barrier((parts, conv_term))
+    send, latent_grad = pack_stage(inputs, parts, conv_term, bias_row, up_send)
 
     following = lax.ppermute(slope_grad[:8], SP, [(i + 1, i) for i in range(count - 1)])
     plane = jnp.sum(lax.all_to_all(send, PLANE, 0, 0, tiled=True).astype(F32), axis=0)

time: 195 us -> 191 us (0.979)
  waiting for transfers between devices: 55.7 us -> 51.5 us
    ppermute x3, waiting for transfers between devices: 26.9 us -> 6.95 us  [turned(): lax.ppermute(block, axis, [(i, (i + distance) % size) for i in range(size)])]
    all_to_all x1, waiting for transfers between devices: 0.01 us -> 15.7 us  [per_device(): lax.all_to_all(key_cot.reshape(count, length, LANES), SP, 0, 0, tiled=True)]
where the time goes in v2:
time: 191 us; the launch traced here: 188 us
  starting transfers between devices  66.6 us (35%)
  waiting for transfers between devices  51.5 us (27%)
  blocking collectives  35 us (18%)
  between operations  14.3 us (7%)
  Pallas kernels  12.3 us (6%)
  local copies, waits for them, and re-layouts  7.31 us (4%)
    ppermute x3, starting transfers between devices, turned(): lax.ppermute(block, axis, [(i, (i + distance) % size) for i in range(size)])  20.1 us
    all_gather x1, blocking collectives, per_device(): lat_all = lax.all_gather(latent, 'zh', axis=0, tiled=True)  19 us
    all_gather x1, blocking collectives, per_device(): lax.all_gather(jnp.concatenate([gate_down, up_mine], axis=0), 'fsdp', axi...  16.1 us
    all_to_all x1, waiting for transfers between devices, per_device(): lax.all_to_all(key_cot.reshape(count, length, LANES), SP, 0, 0, tiled=True)  15.7 us
    all_to_all x1, starting transfers between devices, per_device(): lax.all_to_all(key_cot.reshape(count, length, LANES), SP, 0, 0, tiled=True)  13.8 us
    ppermute x1, waiting for transfers between devices, per_device(): lax.ppermute(projected[length - 8:], SP, [(i, i + 1) for i in range(count...  10.9 us
    all_to_all x1, waiting for transfers between devices, per_device(): lax.all_to_all(send, PLANE, 0, 0, tiled=True).astype(F32)  10 us
    all_to_all x1, starting transfers between devices, per_device(): lax.all_to_all(send, PLANE, 0, 0, tiled=True).astype(F32)  9.18 us
  transfers between devices with their start and end apart: 11, of which 6 were waited for; matrix products, arithmetic and copies ran while one was open for 1% of the time, Pallas kernels for 6%

profile of v2, /device:TPU:1, one launch (start us, length us, event | category | flops | bytes accessed | tf_op | source)
XLA Modules:
  0.0 188.2 jit_solution(9607836042046004812)
XLA Ops:
  7.2 0.7 all-gather.3.cloned.1.call-update
  7.9 0.5 copy-done.7
  8.4 1.1 copy.29
  9.5 7.5 %all-to-all-start = ((bf16[8,512,128]{2,1,0:T(8,128)(2,1)}), bf16[8,512,128]{2,1,0:T(8,128)(2,1)S(1)}, u32[]{:S(2)}, u32[]{:S(2)}) async-start(bf16[8,512,128]{2,1,0:T(8,128)(2,1)} %bitcast.4), calls=%async_computation | async-start | bytes 2097152 | tf_op jit(solution)/shard_map/all_to_all | solution.py:256
  17.2 16.1 %all-gather = bf16[2176,128]{1,0:T(8,128)(2,1)S(1)} all-gather(bf16[272,128]{1,0:T(8,128)(2,1)S(1)} %pad_maximum_fusion.1), channel_id=2, replica_groups=mesh['xl'=2,'zh'=4,'zl'=4,'fsdp'=8,'dp'=2] {'fsdp'}, dimensions={0}, use_global_device_ids=true | all-gather | bytes 626688 | tf_op jit(solution)/shard_map/all_gather | solution.py:264
  33.3 0.2 fusion
  33.6 19.0 %all_gather.14.lat_ref = bf16[512,128]{1,0:T(8,128)(2,1)S(1)} all-gather(bf16[128,128]{1,0:T(8,128)(2,1)S(1)} %fusion), channel_id=1, replica_groups=mesh['xl'=2,'zh'=4,'zl'=4,'fsdp'=8,'dp'=2] {'zh'}, dimensions={0}, use_global_device_ids=true | all-gather | bytes 163840 | tf_op jit(solution)/shard_map/all_gather | solution.py:270
  52.5 1.1 gate_stage.1
  53.7 13.8 %all-to-all-start.1 = ((bf16[32,128,128]{2,1,0:T(8,128)(2,1)}), bf16[32,128,128]{2,1,0:T(8,128)(2,1)S(1)}, u32[]{:S(2)}, u32[]{:S(2)}) async-start(bf16[32,128,128]{2,1,0:T(8,128)(2,1)} %bitcast.50), calls=%async_computation.1 | async-start | bytes 2097152 | tf_op jit(solution)/shard_map/all_to_all | solution.py:276
  67.5 3.1 %collective-permute-start.3 = (bf16[8,4096]{1,0:T(8,128)(2,1)S(1)}, bf16[8,4096]{1,0:T(8,128)(2,1)S(1)}, u32[]{:S(2)}, u32[]{:S(2)}) collective-permute-start(bf16[8,4096]{1,0:T(8,128)(2,1)S(1)} %slice_bitcast_fusion), channel_id=1, source_target_pairs={{0,16},{16,32},{32,48},{48,64},{64,80},{80,96},{96,112},{112,128},... | collective-permute-start | bytes 196616 | tf_op jit(solution)/shard_map/ppermute | solution.py:259
  70.7 7.0 %collective-permute-start = (bf16[128,128]{1,0:T(8,128)(2,1)S(1)}, bf16[128,128]{1,0:T(8,128)(2,1)S(1)}, u32[]{:S(2)}, u32[]{:S(2)}) collective-permute-start(bf16[128,128]{1,0:T(8,128)(2,1)S(1)} %get-tuple-element.36), channel_id=1, source_target_pairs={{0,64},{64,128},{128,192},{192,0},{1,65},{65,129},{129,193},{193,1... | collective-permute-start | bytes 98312 | tf_op jit(solution)/shard_map/ppermute | solution.py:242
  77.7 6.1 %collective-permute-start.1 = (bf16[128,128]{1,0:T(8,128)(2,1)S(1)}, bf16[128,128]{1,0:T(8,128)(2,1)S(1)}, u32[]{:S(2)}, u32[]{:S(2)}) collective-permute-start(bf16[128,128]{1,0:T(8,128)(2,1)S(1)} %get-tuple-element.37), channel_id=1, source_target_pairs={{0,128},{64,192},{128,0},{192,64},{1,129},{65,193},{129,1},{193,65... | collective-permute-start | bytes 98312 | tf_op jit(solution)/shard_map/ppermute | solution.py:242
  83.8 7.0 %collective-permute-start.2 = (bf16[128,128]{1,0:T(8,128)(2,1)S(1)}, bf16[128,128]{1,0:T(8,128)(2,1)S(1)}, u32[]{:S(2)}, u32[]{:S(2)}) collective-permute-start(bf16[128,128]{1,0:T(8,128)(2,1)S(1)} %get-tuple-element.38), channel_id=1, source_target_pairs={{0,192},{64,0},{128,64},{192,128},{1,193},{65,1},{129,65},{193,129... | collective-permute-start | bytes 98312 | tf_op jit(solution)/shard_map/ppermute | solution.py:242
  90.8 10.9 %collective-permute-done.3.before_ref = bf16[8,4096]{1,0:T(8,128)(2,1)S(1)} collective-permute-done((bf16[8,4096]{1,0:T(8,128)(2,1)S(1)}, bf16[8,4096]{1,0:T(8,128)(2,1)S(1)}, u32[]{:S(2)}, u32[]{:S(2)}) %collective-permute-start.3) | collective-permute-done | bytes 65568 | tf_op jit(solution)/shard_map/ppermute | solution.py:259
  101.7 15.7 %all-to-all-done.1.cot_ref = bf16[32,128,128]{2,1,0:T(8,128)(2,1)S(1)} async-done(((bf16[32,128,128]{2,1,0:T(8,128)(2,1)}), bf16[32,128,128]{2,1,0:T(8,128)(2,1)S(1)}, u32[]{:S(2)}, u32[]{:S(2)}) %all-to-all-start.1) | async-done | bytes 1048608 | tf_op jit(solution)/shard_map/all_to_all | solution.py:276
  117.4 3.2 %key_stage.1 = (bf16[128,4096]{1,0:T(8,128)(2,1)S(1)}, f32[32,4,128]{2,1,0:T(4,128)S(1)}) custom-call(bf16[32,128,128]{2,1,0:T(8,128)(2,1)S(1)} %all-to-all-done.1.cot_ref, bf16[128,4096]{1,0:T(8,128)(2,1)S(1)} %bitcast.39, bf16[8,4096]{1,0:T(8,128)(2,1)S(1)} %collective-permute-done.3.before_ref, bf16[4,4096]{1,0:T(4,128)(2,1)S(1)} %copy-done.3), custom_call_target="tpu_custom_call" | custom-call | flops 20971520 | bytes 3145728 | tf_op jit(solution)/shard_map/key_stage/pallas_call | solution.py:44
  120.7 1.0 copy-done.4
  121.7 6.9 %collective-permute-done.1.part2 = bf16[128,128]{1,0:T(8,128)(2,1)S(1)} collective-permute-done((bf16[128,128]{1,0:T(8,128)(2,1)S(1)}, bf16[128,128]{1,0:T(8,128)(2,1)S(1)}, u32[]{:S(2)}, u32[]{:S(2)}) %collective-permute-start.1) | collective-permute-done | bytes 32800 | tf_op jit(solution)/shard_map/ppermute | solution.py:242
  128.6 1.1 pack_stage.1
  129.8 9.2 %all-to-all-start.2 = ((bf16[32,80,128]{2,1,0:T(8,128)(2,1)}), bf16[32,80,128]{2,1,0:T(8,128)(2,1)S(1)}, u32[]{:S(2)}, u32[]{:S(2)}) async-start(bf16[32,80,128]{2,1,0:T(8,128)(2,1)} %get-tuple-element.48), calls=%async_computation.2 | async-start | bytes 1310720 | tf_op jit(solution)/shard_map/all_to_all | solution.py:286
  139.1 1.3 collective-permute-start.4
  140.4 10.0 %all-to-all-done.2 = bf16[32,80,128]{2,1,0:T(8,128)(2,1)S(1)} async-done(((bf16[32,80,128]{2,1,0:T(8,128)(2,1)}), bf16[32,80,128]{2,1,0:T(8,128)(2,1)S(1)}, u32[]{:S(2)}, u32[]{:S(2)}) %all-to-all-start.2) | async-done | bytes 655392 | tf_op jit(solution)/shard_map/all_to_all | solution.py:286
  150.5 0.1 convert_reduce_fusion
  150.7 0.7 pad_maximum_fusion
  151.4 4.8 %all-to-all-start.3 = ((bf16[16,49,128]{2,1,0:T(8,128)(2,1)}), bf16[16,49,128]{2,1,0:T(8,128)(2,1)S(1)}, u32[]{:S(2)}, u32[]{:S(2)}) async-start(bf16[16,49,128]{2,1,0:T(8,128)(2,1)} %pad_maximum_fusion), calls=%async_computation.3 | async-start | bytes 458752 | tf_op jit(solution)/shard_map/all_to_all | solution.py:293
  156.2 3.7 %copy-done.6 = bf16[1152,4096]{1,0:T(8,128)(2,1)S(1)} copy-done((bf16[1152,4096]{1,0:T(8,128)(2,1)S(1)}, bf16[1152,4096]{1,0:T(8,128)(2,1)}, u32[]{:S(2)}) %copy-start.6) | copy-done | bytes 9437208
  159.9 6.1 %input_stage.1 = bf16[128,1152]{1,0:T(8,128)(2,1)} custom-call(bf16[128,4096]{1,0:T(8,128)(2,1)S(1)} %copy-done.5, bf16[8,4096]{1,0:T(8,128)(2,1)S(1)} %collective-permute-done.4.after_ref, bf16[4,4096]{1,0:T(4,128)(2,1)S(1)} %copy-done.3, bf16[1152,4096]{1,0:T(8,128)(2,1)S(1)} %copy-done.6, bf16[128,128]{1,0:T(8,128)(2,1)S(1)} %get-tuple-element.50.latent_ref, ...), custom_call_target="tpu_custom_call" | custom-call | flops 24159191040 | bytes 83886080 | tf_op jit(solution)/shard_map/input_stage/pallas_call | solution.py:189
  166.0 2.8 %all-to-all-done.3 = bf16[16,49,128]{2,1,0:T(8,128)(2,1)S(1)} async-done(((bf16[16,49,128]{2,1,0:T(8,128)(2,1)}), bf16[16,49,128]{2,1,0:T(8,128)(2,1)S(1)}, u32[]{:S(2)}, u32[]{:S(2)}) %all-to-all-start.3) | async-done | bytes 200736 | tf_op jit(solution)/shard_map/all_to_all | solution.py:293
  168.8 0.6 broadcast_in_dim.53
  169.5 6.8 %all-to-all-start.4 = ((f32[4,49,128]{2,1,0:T(8,128)}), f32[4,49,128]{2,1,0:T(8,128)S(1)}, u32[]{:S(2)}, u32[]{:S(2)}) async-start(f32[4,49,128]{2,1,0:T(8,128)} %broadcast_in_dim.53), calls=%async_computation.4 | async-start | bytes 229376 | tf_op jit(solution)/shard_map/all_to_all | solution.py:301
  176.2 4.4 %all-to-all-done.4.shares_ref = f32[4,49,128]{2,1,0:T(8,128)S(1)} async-done(((f32[4,49,128]{2,1,0:T(8,128)}), f32[4,49,128]{2,1,0:T(8,128)S(1)}, u32[]{:S(2)}, u32[]{:S(2)}) %all-to-all-start.4) | async-done | bytes 100384 | tf_op jit(solution)/shard_map/all_to_all | solution.py:301
  180.7 0.6 finish_stage.1
  (43 shorter events, 0.6 us)
Async XLA Ops:
  7.2 45.4 %copy-start = (f32[4096]{0:T(1024)S(1)}, f32[4096]{0:T(1024)}, u32[]{:S(2)}) copy-start(f32[4096]{0:T(1024)} %param.16) | copy-start | bytes 49156
  7.2 1.2 copy-start.7
  7.2 149.0 %all-gather.3.cloned.1.call-start = ((), (), s32[]{:S(2)}) async-start(), calls=%async_computation.5 | async-start | bytes 10616832 | tf_op jit(solution)/shard_map/all_gather | solution.py:260
  9.5 7.5 %copy-start.8 = (bf16[16,4096]{1,0:T(8,128)(2,1)S(1)}, bf16[16,4096]{1,0:T(8,128)(2,1)}, u32[]{:S(2)}) copy-start(bf16[16,4096]{1,0:T(8,128)(2,1)} %param.15) | copy-start | bytes 393220
  9.5 7.7 %copy-start.9 = (bf16[144,128]{1,0:T(8,128)(2,1)S(1)}, bf16[144,128]{1,0:T(8,128)(2,1)}, u32[]{:S(2)}) copy-start(bf16[144,128]{1,0:T(8,128)(2,1)} %param.14) | copy-start | bytes 110596
  9.5 43.0 %all-to-all-start = ((bf16[8,512,128]{2,1,0:T(8,128)(2,1)}), bf16[8,512,128]{2,1,0:T(8,128)(2,1)S(1)}, u32[]{:S(2)}, u32[]{:S(2)}) async-start(bf16[8,512,128]{2,1,0:T(8,128)(2,1)} %bitcast.4), calls=%async_computation | async-start | bytes 2097152 | tf_op jit(solution)/shard_map/all_to_all | solution.py:256
  17.0 16.3 %copy-start.2 = (bf16[1,128,1152]{2,1,0:T(8,128)(2,1)S(1)}, bf16[1,128,1152]{2,1,0:T(8,128)(2,1)}, u32[]{:S(2)}) copy-start(bf16[1,128,1152]{2,1,0:T(8,128)(2,1)} %param.9) | copy-start | bytes 884740
  53.7 13.8 %copy-start.1 = (bf16[1,128,4096]{2,1,0:T(8,128)(2,1)S(1)}, bf16[1,128,4096]{2,1,0:T(8,128)(2,1)}, u32[]{:S(2)}) copy-start(bf16[1,128,4096]{2,1,0:T(8,128)(2,1)} %param.10) | copy-start | bytes 3145732
  53.7 63.7 %copy-start.3 = (bf16[4,4096]{1,0:T(4,128)(2,1)S(1)}, bf16[4,4096]{1,0:T(4,128)(2,1)}, u32[]{:S(2)}) copy-start(bf16[4,4096]{1,0:T(4,128)(2,1)} %taps_ref.3) | copy-start | bytes 98308
  53.7 63.7 %all-to-all-start.1 = ((bf16[32,128,128]{2,1,0:T(8,128)(2,1)}), bf16[32,128,128]{2,1,0:T(8,128)(2,1)S(1)}, u32[]{:S(2)}, u32[]{:S(2)}) async-start(bf16[32,128,128]{2,1,0:T(8,128)(2,1)} %bitcast.50), calls=%async_computation.1 | async-start | bytes 2097152 | tf_op jit(solution)/shard_map/all_to_all | solution.py:276
  67.5 34.2 %collective-permute-start.3 = (bf16[8,4096]{1,0:T(8,128)(2,1)S(1)}, bf16[8,4096]{1,0:T(8,128)(2,1)S(1)}, u32[]{:S(2)}, u32[]{:S(2)}) collective-permute-start(bf16[8,4096]{1,0:T(8,128)(2,1)S(1)} %slice_bitcast_fusion), channel_id=1, source_target_pairs={{0,16},{16,32},{32,48},{48,64},{64,80},{80,96},{96,112},{112,128},... | collective-permute-start | bytes 196616 | tf_op jit(solution)/shard_map/ppermute | solution.py:259
  70.7 51.0 %collective-permute-start = (bf16[128,128]{1,0:T(8,128)(2,1)S(1)}, bf16[128,128]{1,0:T(8,128)(2,1)S(1)}, u32[]{:S(2)}, u32[]{:S(2)}) collective-permute-start(bf16[128,128]{1,0:T(8,128)(2,1)S(1)} %get-tuple-element.36), channel_id=1, source_target_pairs={{0,64},{64,128},{128,192},{192,0},{1,65},{65,129},{129,193},{193,1... | collective-permute-start | bytes 98312 | tf_op jit(solution)/shard_map/ppermute | solution.py:242
  77.7 51.0 %collective-permute-start.1 = (bf16[128,128]{1,0:T(8,128)(2,1)S(1)}, bf16[128,128]{1,0:T(8,128)(2,1)S(1)}, u32[]{:S(2)}, u32[]{:S(2)}) collective-permute-start(bf16[128,128]{1,0:T(8,128)(2,1)S(1)} %get-tuple-element.37), channel_id=1, source_target_pairs={{0,128},{64,192},{128,0},{192,64},{1,129},{65,193},{129,1},{193,65... | collective-permute-start | bytes 98312 | tf_op jit(solution)/shard_map/ppermute | solution.py:242
  83.8 44.9 %collective-permute-start.2 = (bf16[128,128]{1,0:T(8,128)(2,1)S(1)}, bf16[128,128]{1,0:T(8,128)(2,1)S(1)}, u32[]{:S(2)}, u32[]{:S(2)}) collective-permute-start(bf16[128,128]{1,0:T(8,128)(2,1)S(1)} %get-tuple-element.38), channel_id=1, source_target_pairs={{0,192},{64,0},{128,64},{192,128},{1,193},{65,1},{129,65},{193,129... | collective-permute-start | bytes 98312 | tf_op jit(solution)/shard_map/ppermute | solution.py:242
  120.7 1.0 copy-start.4
  121.7 17.5 %copy-start.5 = (bf16[128,4096]{1,0:T(8,128)(2,1)S(1)}, bf16[128,4096]{1,0:T(8,128)(2,1)}, u32[]{:S(2)}) copy-start(bf16[128,4096]{1,0:T(8,128)(2,1)} %copy-done.4) | copy-start | bytes 3145732
  129.8 20.7 %all-to-all-start.2 = ((bf16[32,80,128]{2,1,0:T(8,128)(2,1)}), bf16[32,80,128]{2,1,0:T(8,128)(2,1)S(1)}, u32[]{:S(2)}, u32[]{:S(2)}) async-start(bf16[32,80,128]{2,1,0:T(8,128)(2,1)} %get-tuple-element.48), calls=%async_computation.2 | async-start | bytes 1310720 | tf_op jit(solution)/shard_map/all_to_all | solution.py:286
  139.1 17.0 %collective-permute-start.4 = (bf16[8,4096]{1,0:T(8,128)(2,1)S(1)}, bf16[8,4096]{1,0:T(8,128)(2,1)S(1)}, u32[]{:S(2)}, u32[]{:S(2)}) collective-permute-start(bf16[8,4096]{1,0:T(8,128)(2,1)S(1)} %slice.27), channel_id=1, source_target_pairs={{16,0},{32,16},{48,32},{64,48},{80,64},{96,80},{112,96},{128,112},... | collective-permute-start | bytes 196616 | tf_op jit(solution)/shard_map/ppermute | solution.py:285
  151.4 17.4 %all-to-all-start.3 = ((bf16[16,49,128]{2,1,0:T(8,128)(2,1)}), bf16[16,49,128]{2,1,0:T(8,128)(2,1)S(1)}, u32[]{:S(2)}, u32[]{:S(2)}) async-start(bf16[16,49,128]{2,1,0:T(8,128)(2,1)} %pad_maximum_fusion), calls=%async_computation.3 | async-start | bytes 458752 | tf_op jit(solution)/shard_map/all_to_all | solution.py:293
  156.2 3.7 %copy-start.6 = (bf16[1152,4096]{1,0:T(8,128)(2,1)S(1)}, bf16[1152,4096]{1,0:T(8,128)(2,1)}, u32[]{:S(2)}) copy-start(bf16[1152,4096]{1,0:T(8,128)(2,1)} %all-gather.3.cloned.1.call-done.key_ref) | copy-start | bytes 28311556
  169.5 11.2 %all-to-all-start.4 = ((f32[4,49,128]{2,1,0:T(8,128)}), f32[4,49,128]{2,1,0:T(8,128)S(1)}, u32[]{:S(2)}, u32[]{:S(2)}) async-start(f32[4,49,128]{2,1,0:T(8,128)} %broadcast_in_dim.53), calls=%async_computation.4 | async-start | bytes 229376 | tf_op jit(solution)/shard_map/all_to_all | solution.py:301
Sparse Core Ops, SparseCore 0:
  10.1 67.5 all-gather.2

commit v3 on v2

--- a/solution.py
+++ b/solution.py
@@ -268,13 +268,14 @@
     up_rows = factors[:, rows_down:].reshape(8, 8, rows_up, LANES)
     latent = jnp.dot(inputs, down_full, preferred_element_type=F32).astype(BF16)
     lat_all = lax.all_gather(latent, "zh", axis=0, tiled=True)
+    lat_all, key_cot = lax.optimization_barrier((lat_all, key_cot))
+    key_seq = lax.all_to_all(key_cot.reshape(count, length, LANES), SP, 0, 0, tiled=True)
     bias_mine = lax.dynamic_index_in_dim(gate_bias.reshape(2, 4, 4, LANES), zh, 1, False)
     *parts, up_send, bias_term = gate_stage(
         zh.astype(jnp.int32).reshape(1), gate_mid, lat_all, up_rows, bias_mine.reshape(8, LANES)
     )
-    parts, key_cot = lax.optimization_barrier((parts, key_cot))
-    key_seq = lax.all_to_all(key_cot.reshape(count, length, LANES), SP, 0, 0, tiled=True)
-    parts = parts[:1] + [turned(parts[k], "zh", k) for k in range(1, 4)]
+    far, ahead, behind = (turned(parts[k], "zh", k) for k in (2, 1, 3))
+    parts = [parts[0], ahead, far, behind]
     bias_row = lax.dynamic_update_slice_in_dim(
         jnp.zeros((2, 4, 4, LANES), F32), bias_term.reshape(2, 1, 4, LANES), zh, 1
     ).reshape(count, 1, LANES)

time: 191 us -> 191 us (level)
  local copies, waits for them, and re-layouts: 7.31 us -> 11.3 us
  waiting for transfers between devices: 51.5 us -> 47.8 us
    ppermute x1, waiting for transfers between devices: 10.9 us -> 7.79 us  [per_device(): lax.ppermute(projected[length - 8:], SP, [(i, i + 1) for i in range(count...]
    unnamed x20 -> x26, local copies, waits for them, and re-layouts: 5.19 us -> 8.2 us
  transfers between devices with their start and end apart: 11 -> 11, of which waited for: 6 -> 6; matrix products, arithmetic and copies ran while one was open for 1% -> 2% of each run, Pallas kernels for 6% -> 6%
where the time goes in v3:
time: 191 us; the launch traced here: 188 us
  starting transfers between devices  65.8 us (34%)
  waiting for transfers between devices  47.8 us (25%)
  blocking collectives  35.2 us (18%)
  between operations  14.3 us (7%)
  Pallas kernels  12.3 us (6%)
  local copies, waits for them, and re-layouts  11.3 us (6%)
    ppermute x3, starting transfers between devices, turned(): lax.ppermute(block, axis, [(i, (i + distance) % size) for i in range(size)])  20.1 us
    all_gather x1, blocking collectives, per_device(): lat_all = lax.all_gather(latent, 'zh', axis=0, tiled=True)  19.1 us
    all_gather x1, blocking collectives, per_device(): lax.all_gather(jnp.concatenate([gate_down, up_mine], axis=0), 'fsdp', axi...  16.1 us
    all_to_all x1, waiting for transfers between devices, per_device(): lax.all_to_all(key_cot.reshape(count, length, LANES), SP, 0, 0, tiled=True)  15.6 us
    all_to_all x1, starting transfers between devices, per_device(): lax.all_to_all(key_cot.reshape(count, length, LANES), SP, 0, 0, tiled=True)  12.2 us
    all_to_all x1, waiting for transfers between devices, per_device(): lax.all_to_all(send, PLANE, 0, 0, tiled=True).astype(F32)  10 us
    all_to_all x1, starting transfers between devices, per_device(): lax.all_to_all(send, PLANE, 0, 0, tiled=True).astype(F32)  10 us
    unnamed x26, local copies, waits for them, and re-layouts  8.2 us
  transfers between devices with their start and end apart: 11, of which 6 were waited for; matrix products, arithmetic and copies ran while one was open for 2% of the time, Pallas kernels for 6%

profile of v3, /device:TPU:1, one launch (start us, length us, event | category | flops | bytes accessed | tf_op | source)
XLA Modules:
  0.0 187.9 jit_solution(7899474180730022166)
XLA Ops:
  7.2 0.7 all-gather.3.cloned.1.call-update
  8.4 1.1 copy.29
  9.5 7.5 %all-to-all-start = ((bf16[8,512,128]{2,1,0:T(8,128)(2,1)}), bf16[8,512,128]{2,1,0:T(8,128)(2,1)S(1)}, u32[]{:S(2)}, u32[]{:S(2)}) async-start(bf16[8,512,128]{2,1,0:T(8,128)(2,1)} %bitcast.4), calls=%async_computation | async-start | bytes 2097152 | tf_op jit(solution)/shard_map/all_to_all | solution.py:256
  17.2 16.1 %all-gather = bf16[2176,128]{1,0:T(8,128)(2,1)S(1)} all-gather(bf16[272,128]{1,0:T(8,128)(2,1)S(1)} %pad_maximum_fusion.1), channel_id=2, replica_groups=mesh['xl'=2,'zh'=4,'zl'=4,'fsdp'=8,'dp'=2] {'fsdp'}, dimensions={0}, use_global_device_ids=true | all-gather | bytes 626688 | tf_op jit(solution)/shard_map/all_gather | solution.py:264
  33.2 0.8 copy-done.9
  34.3 19.1 %all_gather.14.lat_ref = bf16[512,128]{1,0:T(8,128)(2,1)S(1)} all-gather(bf16[128,128]{1,0:T(8,128)(2,1)S(1)} %fusion), channel_id=1, replica_groups=mesh['xl'=2,'zh'=4,'zl'=4,'fsdp'=8,'dp'=2] {'zh'}, dimensions={0}, use_global_device_ids=true | all-gather | bytes 163840 | tf_op jit(solution)/shard_map/all_gather | solution.py:270
  53.4 1.0 copy-done.3
  54.4 12.2 %all-to-all-start.1 = ((bf16[32,128,128]{2,1,0:T(8,128)(2,1)}), bf16[32,128,128]{2,1,0:T(8,128)(2,1)S(1)}, u32[]{:S(2)}, u32[]{:S(2)}) async-start(bf16[32,128,128]{2,1,0:T(8,128)(2,1)} %bitcast.50), calls=%async_computation.1 | async-start | bytes 2097152 | tf_op jit(solution)/shard_map/all_to_all | solution.py:272
  66.6 3.1 %collective-permute-start.3 = (bf16[8,4096]{1,0:T(8,128)(2,1)S(1)}, bf16[8,4096]{1,0:T(8,128)(2,1)S(1)}, u32[]{:S(2)}, u32[]{:S(2)}) collective-permute-start(bf16[8,4096]{1,0:T(8,128)(2,1)S(1)} %slice_bitcast_fusion), channel_id=1, source_target_pairs={{0,16},{16,32},{32,48},{48,64},{64,80},{80,96},{96,112},{112,128},... | collective-permute-start | bytes 196616 | tf_op jit(solution)/shard_map/ppermute | solution.py:259
  69.8 1.0 slice.29
  70.8 1.2 copy-done.4
  72.0 1.2 gate_stage.1
  73.2 7.0 %collective-permute-start = (bf16[128,128]{1,0:T(8,128)(2,1)S(1)}, bf16[128,128]{1,0:T(8,128)(2,1)S(1)}, u32[]{:S(2)}, u32[]{:S(2)}) collective-permute-start(bf16[128,128]{1,0:T(8,128)(2,1)S(1)} %get-tuple-element.30), channel_id=1, source_target_pairs={{0,64},{64,128},{128,192},{192,0},{1,65},{65,129},{129,193},{193,1... | collective-permute-start | bytes 98312 | tf_op jit(solution)/shard_map/ppermute | solution.py:242
  80.2 6.1 %collective-permute-start.1 = (bf16[128,128]{1,0:T(8,128)(2,1)S(1)}, bf16[128,128]{1,0:T(8,128)(2,1)S(1)}, u32[]{:S(2)}, u32[]{:S(2)}) collective-permute-start(bf16[128,128]{1,0:T(8,128)(2,1)S(1)} %get-tuple-element.31), channel_id=1, source_target_pairs={{0,128},{64,192},{128,0},{192,64},{1,129},{65,193},{129,1},{193,65... | collective-permute-start | bytes 98312 | tf_op jit(solution)/shard_map/ppermute | solution.py:242
  86.3 7.0 %collective-permute-start.2 = (bf16[128,128]{1,0:T(8,128)(2,1)S(1)}, bf16[128,128]{1,0:T(8,128)(2,1)S(1)}, u32[]{:S(2)}, u32[]{:S(2)}) collective-permute-start(bf16[128,128]{1,0:T(8,128)(2,1)S(1)} %get-tuple-element.32), channel_id=1, source_target_pairs={{0,192},{64,0},{128,64},{192,128},{1,193},{65,1},{129,65},{193,129... | collective-permute-start | bytes 98312 | tf_op jit(solution)/shard_map/ppermute | solution.py:242
  93.3 7.8 %collective-permute-done.3.before_ref = bf16[8,4096]{1,0:T(8,128)(2,1)S(1)} collective-permute-done((bf16[8,4096]{1,0:T(8,128)(2,1)S(1)}, bf16[8,4096]{1,0:T(8,128)(2,1)S(1)}, u32[]{:S(2)}, u32[]{:S(2)}) %collective-permute-start.3) | collective-permute-done | bytes 65568 | tf_op jit(solution)/shard_map/ppermute | solution.py:259
  101.1 15.6 %all-to-all-done.1.cot_ref = bf16[32,128,128]{2,1,0:T(8,128)(2,1)S(1)} async-done(((bf16[32,128,128]{2,1,0:T(8,128)(2,1)}), bf16[32,128,128]{2,1,0:T(8,128)(2,1)S(1)}, u32[]{:S(2)}, u32[]{:S(2)}) %all-to-all-start.1) | async-done | bytes 1048608 | tf_op jit(solution)/shard_map/all_to_all | solution.py:272
  116.8 3.2 %key_stage.1 = (bf16[128,4096]{1,0:T(8,128)(2,1)S(1)}, f32[32,4,128]{2,1,0:T(4,128)S(1)}) custom-call(bf16[32,128,128]{2,1,0:T(8,128)(2,1)S(1)} %all-to-all-done.1.cot_ref, bf16[128,4096]{1,0:T(8,128)(2,1)S(1)} %bitcast.39, bf16[8,4096]{1,0:T(8,128)(2,1)S(1)} %collective-permute-done.3.before_ref, bf16[4,4096]{1,0:T(4,128)(2,1)S(1)} %copy-done.5), custom_call_target="tpu_custom_call" | custom-call | flops 20971520 | bytes 3145728 | tf_op jit(solution)/shard_map/key_stage/pallas_call | solution.py:44
  120.0 1.0 copy-done.6
  121.0 6.5 %collective-permute-done.1.part2 = bf16[128,128]{1,0:T(8,128)(2,1)S(1)} collective-permute-done((bf16[128,128]{1,0:T(8,128)(2,1)S(1)}, bf16[128,128]{1,0:T(8,128)(2,1)S(1)}, u32[]{:S(2)}, u32[]{:S(2)}) %collective-permute-start.1) | collective-permute-done | bytes 32800 | tf_op jit(solution)/shard_map/ppermute | solution.py:242
  127.5 1.1 pack_stage.1
  128.6 10.0 %all-to-all-start.2 = ((bf16[32,80,128]{2,1,0:T(8,128)(2,1)}), bf16[32,80,128]{2,1,0:T(8,128)(2,1)S(1)}, u32[]{:S(2)}, u32[]{:S(2)}) async-start(bf16[32,80,128]{2,1,0:T(8,128)(2,1)} %get-tuple-element.42), calls=%async_computation.2 | async-start | bytes 1310720 | tf_op jit(solution)/shard_map/all_to_all | solution.py:287
  138.8 1.3 collective-permute-start.4
  140.1 10.0 %all-to-all-done.2 = bf16[32,80,128]{2,1,0:T(8,128)(2,1)S(1)} async-done(((bf16[32,80,128]{2,1,0:T(8,128)(2,1)}), bf16[32,80,128]{2,1,0:T(8,128)(2,1)S(1)}, u32[]{:S(2)}, u32[]{:S(2)}) %all-to-all-start.2) | async-done | bytes 655392 | tf_op jit(solution)/shard_map/all_to_all | solution.py:287
  150.4 0.7 pad_maximum_fusion
  151.1 4.8 %all-to-all-start.3 = ((bf16[16,49,128]{2,1,0:T(8,128)(2,1)}), bf16[16,49,128]{2,1,0:T(8,128)(2,1)S(1)}, u32[]{:S(2)}, u32[]{:S(2)}) async-start(bf16[16,49,128]{2,1,0:T(8,128)(2,1)} %pad_maximum_fusion), calls=%async_computation.3 | async-start | bytes 458752 | tf_op jit(solution)/shard_map/all_to_all | solution.py:294
  155.9 3.7 %copy-done.8 = bf16[1152,4096]{1,0:T(8,128)(2,1)S(1)} copy-done((bf16[1152,4096]{1,0:T(8,128)(2,1)S(1)}, bf16[1152,4096]{1,0:T(8,128)(2,1)}, u32[]{:S(2)}) %copy-start.8) | copy-done | bytes 9437208
  159.6 6.1 %input_stage.1 = bf16[128,1152]{1,0:T(8,128)(2,1)} custom-call(bf16[128,4096]{1,0:T(8,128)(2,1)S(1)} %copy-done.7, bf16[8,4096]{1,0:T(8,128)(2,1)S(1)} %collective-permute-done.4.after_ref, bf16[4,4096]{1,0:T(4,128)(2,1)S(1)} %copy-done.5, bf16[1152,4096]{1,0:T(8,128)(2,1)S(1)} %copy-done.8, bf16[128,128]{1,0:T(8,128)(2,1)S(1)} %get-tuple-element.44.latent_ref, ...), custom_call_target="tpu_custom_call" | custom-call | flops 24159191040 | bytes 83886080 | tf_op jit(solution)/shard_map/input_stage/pallas_call | solution.py:189
  165.7 2.8 %all-to-all-done.3 = bf16[16,49,128]{2,1,0:T(8,128)(2,1)S(1)} async-done(((bf16[16,49,128]{2,1,0:T(8,128)(2,1)}), bf16[16,49,128]{2,1,0:T(8,128)(2,1)S(1)}, u32[]{:S(2)}, u32[]{:S(2)}) %all-to-all-start.3) | async-done | bytes 200736 | tf_op jit(solution)/shard_map/all_to_all | solution.py:294
  168.5 0.7 broadcast_in_dim.53
  169.1 6.8 %all-to-all-start.4 = ((f32[4,49,128]{2,1,0:T(8,128)}), f32[4,49,128]{2,1,0:T(8,128)S(1)}, u32[]{:S(2)}, u32[]{:S(2)}) async-start(f32[4,49,128]{2,1,0:T(8,128)} %broadcast_in_dim.53), calls=%async_computation.4 | async-start | bytes 229376 | tf_op jit(solution)/shard_map/all_to_all | solution.py:302
  175.9 4.4 %all-to-all-done.4.shares_ref = f32[4,49,128]{2,1,0:T(8,128)S(1)} async-done(((f32[4,49,128]{2,1,0:T(8,128)}), f32[4,49,128]{2,1,0:T(8,128)S(1)}, u32[]{:S(2)}, u32[]{:S(2)}) %all-to-all-start.4) | async-done | bytes 100384 | tf_op jit(solution)/shard_map/all_to_all | solution.py:302
  (49 shorter events, 2.1 us)
Async XLA Ops:
  7.2 63.6 %copy-start = (f32[4096]{0:T(1024)S(1)}, f32[4096]{0:T(1024)}, u32[]{:S(2)}) copy-start(f32[4096]{0:T(1024)} %param.16) | copy-start | bytes 49156
  7.2 1.2 copy-start.10
  7.2 148.7 %all-gather.3.cloned.1.call-start = ((), (), s32[]{:S(2)}) async-start(), calls=%async_computation.5 | async-start | bytes 10616832 | tf_op jit(solution)/shard_map/all_gather | solution.py:260
  9.5 7.5 %copy-start.11 = (bf16[16,4096]{1,0:T(8,128)(2,1)S(1)}, bf16[16,4096]{1,0:T(8,128)(2,1)}, u32[]{:S(2)}) copy-start(bf16[16,4096]{1,0:T(8,128)(2,1)} %param.15) | copy-start | bytes 393220
  9.5 7.7 %copy-start.12 = (bf16[144,128]{1,0:T(8,128)(2,1)S(1)}, bf16[144,128]{1,0:T(8,128)(2,1)}, u32[]{:S(2)}) copy-start(bf16[144,128]{1,0:T(8,128)(2,1)} %param.14) | copy-start | bytes 110596
  9.5 43.9 %all-to-all-start = ((bf16[8,512,128]{2,1,0:T(8,128)(2,1)}), bf16[8,512,128]{2,1,0:T(8,128)(2,1)S(1)}, u32[]{:S(2)}, u32[]{:S(2)}) async-start(bf16[8,512,128]{2,1,0:T(8,128)(2,1)} %bitcast.4), calls=%async_computation | async-start | bytes 2097152 | tf_op jit(solution)/shard_map/all_to_all | solution.py:256
  17.0 17.0 %copy-start.2 = (bf16[1,128,1152]{2,1,0:T(8,128)(2,1)S(1)}, bf16[1,128,1152]{2,1,0:T(8,128)(2,1)}, u32[]{:S(2)}) copy-start(bf16[1,128,1152]{2,1,0:T(8,128)(2,1)} %param.9) | copy-start | bytes 884740
  33.2 0.8 copy-start.9
  34.0 32.6 %copy-start.1 = (bf16[1,128,4096]{2,1,0:T(8,128)(2,1)S(1)}, bf16[1,128,4096]{2,1,0:T(8,128)(2,1)}, u32[]{:S(2)}) copy-start(bf16[1,128,4096]{2,1,0:T(8,128)(2,1)} %param.10) | copy-start | bytes 3145732
  53.4 1.0 copy-start.3
  54.4 62.4 %all-to-all-start.1 = ((bf16[32,128,128]{2,1,0:T(8,128)(2,1)}), bf16[32,128,128]{2,1,0:T(8,128)(2,1)S(1)}, u32[]{:S(2)}, u32[]{:S(2)}) async-start(bf16[32,128,128]{2,1,0:T(8,128)(2,1)} %bitcast.50), calls=%async_computation.1 | async-start | bytes 2097152 | tf_op jit(solution)/shard_map/all_to_all | solution.py:272
  66.6 50.2 %copy-start.5 = (bf16[4,4096]{1,0:T(4,128)(2,1)S(1)}, bf16[4,4096]{1,0:T(4,128)(2,1)}, u32[]{:S(2)}) copy-start(bf16[4,4096]{1,0:T(4,128)(2,1)} %taps_ref.3) | copy-start | bytes 98308
  66.6 34.5 %collective-permute-start.3 = (bf16[8,4096]{1,0:T(8,128)(2,1)S(1)}, bf16[8,4096]{1,0:T(8,128)(2,1)S(1)}, u32[]{:S(2)}, u32[]{:S(2)}) collective-permute-start(bf16[8,4096]{1,0:T(8,128)(2,1)S(1)} %slice_bitcast_fusion), channel_id=1, source_target_pairs={{0,16},{16,32},{32,48},{48,64},{64,80},{80,96},{96,112},{112,128},... | collective-permute-start | bytes 196616 | tf_op jit(solution)/shard_map/ppermute | solution.py:259
  70.8 1.2 copy-start.4
  73.2 47.8 %collective-permute-start = (bf16[128,128]{1,0:T(8,128)(2,1)S(1)}, bf16[128,128]{1,0:T(8,128)(2,1)S(1)}, u32[]{:S(2)}, u32[]{:S(2)}) collective-permute-start(bf16[128,128]{1,0:T(8,128)(2,1)S(1)} %get-tuple-element.30), channel_id=1, source_target_pairs={{0,64},{64,128},{128,192},{192,0},{1,65},{65,129},{129,193},{193,1... | collective-permute-start | bytes 98312 | tf_op jit(solution)/shard_map/ppermute | solution.py:242
  80.2 47.3 %collective-permute-start.1 = (bf16[128,128]{1,0:T(8,128)(2,1)S(1)}, bf16[128,128]{1,0:T(8,128)(2,1)S(1)}, u32[]{:S(2)}, u32[]{:S(2)}) collective-permute-start(bf16[128,128]{1,0:T(8,128)(2,1)S(1)} %get-tuple-element.31), channel_id=1, source_target_pairs={{0,128},{64,192},{128,0},{192,64},{1,129},{65,193},{129,1},{193,65... | collective-permute-start | bytes 98312 | tf_op jit(solution)/shard_map/ppermute | solution.py:242
  86.3 41.2 %collective-permute-start.2 = (bf16[128,128]{1,0:T(8,128)(2,1)S(1)}, bf16[128,128]{1,0:T(8,128)(2,1)S(1)}, u32[]{:S(2)}, u32[]{:S(2)}) collective-permute-start(bf16[128,128]{1,0:T(8,128)(2,1)S(1)} %get-tuple-element.32), channel_id=1, source_target_pairs={{0,192},{64,0},{128,64},{192,128},{1,193},{65,1},{129,65},{193,129... | collective-permute-start | bytes 98312 | tf_op jit(solution)/shard_map/ppermute | solution.py:242
  120.0 1.0 copy-start.6
  121.0 17.8 %copy-start.7 = (bf16[128,4096]{1,0:T(8,128)(2,1)S(1)}, bf16[128,4096]{1,0:T(8,128)(2,1)}, u32[]{:S(2)}) copy-start(bf16[128,4096]{1,0:T(8,128)(2,1)} %copy-done.6) | copy-start | bytes 3145732
  128.6 21.5 %all-to-all-start.2 = ((bf16[32,80,128]{2,1,0:T(8,128)(2,1)}), bf16[32,80,128]{2,1,0:T(8,128)(2,1)S(1)}, u32[]{:S(2)}, u32[]{:S(2)}) async-start(bf16[32,80,128]{2,1,0:T(8,128)(2,1)} %get-tuple-element.42), calls=%async_computation.2 | async-start | bytes 1310720 | tf_op jit(solution)/shard_map/all_to_all | solution.py:287
  138.8 17.0 %collective-permute-start.4 = (bf16[8,4096]{1,0:T(8,128)(2,1)S(1)}, bf16[8,4096]{1,0:T(8,128)(2,1)S(1)}, u32[]{:S(2)}, u32[]{:S(2)}) collective-permute-start(bf16[8,4096]{1,0:T(8,128)(2,1)S(1)} %slice.27), channel_id=1, source_target_pairs={{16,0},{32,16},{48,32},{64,48},{80,64},{96,80},{112,96},{128,112},... | collective-permute-start | bytes 196616 | tf_op jit(solution)/shard_map/ppermute | solution.py:286
  151.1 17.4 %all-to-all-start.3 = ((bf16[16,49,128]{2,1,0:T(8,128)(2,1)}), bf16[16,49,128]{2,1,0:T(8,128)(2,1)S(1)}, u32[]{:S(2)}, u32[]{:S(2)}) async-start(bf16[16,49,128]{2,1,0:T(8,128)(2,1)} %pad_maximum_fusion), calls=%async_computation.3 | async-start | bytes 458752 | tf_op jit(solution)/shard_map/all_to_all | solution.py:294
  155.9 3.7 %copy-start.8 = (bf16[1152,4096]{1,0:T(8,128)(2,1)S(1)}, bf16[1152,4096]{1,0:T(8,128)(2,1)}, u32[]{:S(2)}) copy-start(bf16[1152,4096]{1,0:T(8,128)(2,1)} %all-gather.3.cloned.1.call-done.key_ref) | copy-start | bytes 28311556
  169.1 11.2 %all-to-all-start.4 = ((f32[4,49,128]{2,1,0:T(8,128)}), f32[4,49,128]{2,1,0:T(8,128)S(1)}, u32[]{:S(2)}, u32[]{:S(2)}) async-start(f32[4,49,128]{2,1,0:T(8,128)} %broadcast_in_dim.53), calls=%async_computation.4 | async-start | bytes 229376 | tf_op jit(solution)/shard_map/all_to_all | solution.py:302
Sparse Core Ops, SparseCore 0:
  10.1 67.5 all-gather.2

commit v4 on v3

--- a/solution.py
+++ b/solution.py
@@ -275,7 +275,7 @@
         zh.astype(jnp.int32).reshape(1), gate_mid, lat_all, up_rows, bias_mine.reshape(8, LANES)
     )
     far, ahead, behind = (turned(parts[k], "zh", k) for k in (2, 1, 3))
-    parts = [parts[0], ahead, far, behind]
+    parts = [parts[0], far, ahead, behind]
     bias_row = lax.dynamic_update_slice_in_dim(
         jnp.zeros((2, 4, 4, LANES), F32), bias_term.reshape(2, 1, 4, LANES), zh, 1
     ).reshape(count, 1, LANES)

time: 191 us -> 191 us (level)
  no operation moved by 1% of the time
where the time goes in v4:
time: 191 us; the launch traced here: 188 us
  starting transfers between devices  67.5 us (35%)
  waiting for transfers between devices  46.2 us (24%)
  blocking collectives  35.2 us (18%)
  between operations  14.3 us (7%)
  Pallas kernels  12.3 us (6%)
  local copies, waits for them, and re-layouts  11.3 us (6%)
    ppermute x3, starting transfers between devices, turned(): lax.ppermute(block, axis, [(i, (i + distance) % size) for i in range(size)])  20.1 us
    all_gather x1, blocking collectives, per_device(): lat_all = lax.all_gather(latent, 'zh', axis=0, tiled=True)  19.1 us
    all_gather x1, blocking collectives, per_device(): lax.all_gather(jnp.concatenate([gate_down, up_mine], axis=0), 'fsdp', axi...  16.1 us
    all_to_all x1, waiting for transfers between devices, per_device(): lax.all_to_all(key_cot.reshape(count, length, LANES), SP, 0, 0, tiled=True)  14.8 us
    all_to_all x1, starting transfers between devices, per_device(): lax.all_to_all(key_cot.reshape(count, length, LANES), SP, 0, 0, tiled=True)  12.2 us
    all_to_all x1, starting transfers between devices, per_device(): lax.all_to_all(send, PLANE, 0, 0, tiled=True).astype(F32)  10.9 us
    all_to_all x1, waiting for transfers between devices, per_device(): lax.all_to_all(send, PLANE, 0, 0, tiled=True).astype(F32)  10 us
    unnamed x26, local copies, waits for them, and re-layouts  8.2 us
  transfers between devices with their start and end apart: 11, of which 6 were waited for; matrix products, arithmetic and copies ran while one was open for 2% of the time, Pallas kernels for 6%

profile of v4, /device:TPU:1, one launch (start us, length us, event | category | flops | bytes accessed | tf_op | source)
XLA Modules:
  0.0 187.9 jit_solution(1859834250545779074)
XLA Ops:
  7.2 0.7 all-gather.3.cloned.1.call-update
  8.4 1.1 copy.29
  9.5 7.5 %all-to-all-start = ((bf16[8,512,128]{2,1,0:T(8,128)(2,1)}), bf16[8,512,128]{2,1,0:T(8,128)(2,1)S(1)}, u32[]{:S(2)}, u32[]{:S(2)}) async-start(bf16[8,512,128]{2,1,0:T(8,128)(2,1)} %bitcast.4), calls=%async_computation | async-start | bytes 2097152 | tf_op jit(solution)/shard_map/all_to_all | solution.py:256
  17.2 16.1 %all-gather = bf16[2176,128]{1,0:T(8,128)(2,1)S(1)} all-gather(bf16[272,128]{1,0:T(8,128)(2,1)S(1)} %pad_maximum_fusion.1), channel_id=2, replica_groups=mesh['xl'=2,'zh'=4,'zl'=4,'fsdp'=8,'dp'=2] {'fsdp'}, dimensions={0}, use_global_device_ids=true | all-gather | bytes 626688 | tf_op jit(solution)/shard_map/all_gather | solution.py:264
  33.2 0.8 copy-done.9
  34.3 19.1 %all_gather.14.lat_ref = bf16[512,128]{1,0:T(8,128)(2,1)S(1)} all-gather(bf16[128,128]{1,0:T(8,128)(2,1)S(1)} %fusion), channel_id=1, replica_groups=mesh['xl'=2,'zh'=4,'zl'=4,'fsdp'=8,'dp'=2] {'zh'}, dimensions={0}, use_global_device_ids=true | all-gather | bytes 163840 | tf_op jit(solution)/shard_map/all_gather | solution.py:270
  53.4 1.0 copy-done.3
  54.4 12.2 %all-to-all-start.1 = ((bf16[32,128,128]{2,1,0:T(8,128)(2,1)}), bf16[32,128,128]{2,1,0:T(8,128)(2,1)S(1)}, u32[]{:S(2)}, u32[]{:S(2)}) async-start(bf16[32,128,128]{2,1,0:T(8,128)(2,1)} %bitcast.50), calls=%async_computation.1 | async-start | bytes 2097152 | tf_op jit(solution)/shard_map/all_to_all | solution.py:272
  66.6 3.1 %collective-permute-start.3 = (bf16[8,4096]{1,0:T(8,128)(2,1)S(1)}, bf16[8,4096]{1,0:T(8,128)(2,1)S(1)}, u32[]{:S(2)}, u32[]{:S(2)}) collective-permute-start(bf16[8,4096]{1,0:T(8,128)(2,1)S(1)} %slice_bitcast_fusion), channel_id=1, source_target_pairs={{0,16},{16,32},{32,48},{48,64},{64,80},{80,96},{96,112},{112,128},... | collective-permute-start | bytes 196616 | tf_op jit(solution)/shard_map/ppermute | solution.py:259
  69.8 1.0 slice.29
  70.8 1.2 copy-done.4
  72.0 1.2 gate_stage.1
  73.2 10.9 %collective-permute-start = (bf16[128,128]{1,0:T(8,128)(2,1)S(1)}, bf16[128,128]{1,0:T(8,128)(2,1)S(1)}, u32[]{:S(2)}, u32[]{:S(2)}) collective-permute-start(bf16[128,128]{1,0:T(8,128)(2,1)S(1)} %get-tuple-element.30), channel_id=1, source_target_pairs={{0,128},{64,192},{128,0},{192,64},{1,129},{65,193},{129,1},{193,65... | collective-permute-start | bytes 98312 | tf_op jit(solution)/shard_map/ppermute | solution.py:242
  84.1 2.2 %collective-permute-start.1 = (bf16[128,128]{1,0:T(8,128)(2,1)S(1)}, bf16[128,128]{1,0:T(8,128)(2,1)S(1)}, u32[]{:S(2)}, u32[]{:S(2)}) collective-permute-start(bf16[128,128]{1,0:T(8,128)(2,1)S(1)} %get-tuple-element.31), channel_id=1, source_target_pairs={{0,64},{64,128},{128,192},{192,0},{1,65},{65,129},{129,193},{193,1... | collective-permute-start | bytes 98312 | tf_op jit(solution)/shard_map/ppermute | solution.py:242
  86.3 7.0 %collective-permute-start.2 = (bf16[128,128]{1,0:T(8,128)(2,1)S(1)}, bf16[128,128]{1,0:T(8,128)(2,1)S(1)}, u32[]{:S(2)}, u32[]{:S(2)}) collective-permute-start(bf16[128,128]{1,0:T(8,128)(2,1)S(1)} %get-tuple-element.32), channel_id=1, source_target_pairs={{0,192},{64,0},{128,64},{192,128},{1,193},{65,1},{129,65},{193,129... | collective-permute-start | bytes 98312 | tf_op jit(solution)/shard_map/ppermute | solution.py:242
  93.3 7.8 %collective-permute-done.3.before_ref = bf16[8,4096]{1,0:T(8,128)(2,1)S(1)} collective-permute-done((bf16[8,4096]{1,0:T(8,128)(2,1)S(1)}, bf16[8,4096]{1,0:T(8,128)(2,1)S(1)}, u32[]{:S(2)}, u32[]{:S(2)}) %collective-permute-start.3) | collective-permute-done | bytes 65568 | tf_op jit(solution)/shard_map/ppermute | solution.py:259
  101.1 14.8 %all-to-all-done.1.cot_ref = bf16[32,128,128]{2,1,0:T(8,128)(2,1)S(1)} async-done(((bf16[32,128,128]{2,1,0:T(8,128)(2,1)}), bf16[32,128,128]{2,1,0:T(8,128)(2,1)S(1)}, u32[]{:S(2)}, u32[]{:S(2)}) %all-to-all-start.1) | async-done | bytes 1048608 | tf_op jit(solution)/shard_map/all_to_all | solution.py:272
  116.0 3.2 %key_stage.1 = (bf16[128,4096]{1,0:T(8,128)(2,1)S(1)}, f32[32,4,128]{2,1,0:T(4,128)S(1)}) custom-call(bf16[32,128,128]{2,1,0:T(8,128)(2,1)S(1)} %all-to-all-done.1.cot_ref, bf16[128,4096]{1,0:T(8,128)(2,1)S(1)} %bitcast.39, bf16[8,4096]{1,0:T(8,128)(2,1)S(1)} %collective-permute-done.3.before_ref, bf16[4,4096]{1,0:T(4,128)(2,1)S(1)} %copy-done.5), custom_call_target="tpu_custom_call" | custom-call | flops 20971520 | bytes 3145728 | tf_op jit(solution)/shard_map/key_stage/pallas_call | solution.py:44
  119.2 1.0 copy-done.6
  120.2 5.6 %collective-permute-done.part1 = bf16[128,128]{1,0:T(8,128)(2,1)S(1)} collective-permute-done((bf16[128,128]{1,0:T(8,128)(2,1)S(1)}, bf16[128,128]{1,0:T(8,128)(2,1)S(1)}, u32[]{:S(2)}, u32[]{:S(2)}) %collective-permute-start) | collective-permute-done | bytes 32800 | tf_op jit(solution)/shard_map/ppermute | solution.py:242
  125.8 1.1 pack_stage.1
  127.0 10.9 %all-to-all-start.2 = ((bf16[32,80,128]{2,1,0:T(8,128)(2,1)}), bf16[32,80,128]{2,1,0:T(8,128)(2,1)S(1)}, u32[]{:S(2)}, u32[]{:S(2)}) async-start(bf16[32,80,128]{2,1,0:T(8,128)(2,1)} %get-tuple-element.42), calls=%async_computation.2 | async-start | bytes 1310720 | tf_op jit(solution)/shard_map/all_to_all | solution.py:287
  138.1 1.3 collective-permute-start.4
  139.4 10.0 %all-to-all-done.2 = bf16[32,80,128]{2,1,0:T(8,128)(2,1)S(1)} async-done(((bf16[32,80,128]{2,1,0:T(8,128)(2,1)}), bf16[32,80,128]{2,1,0:T(8,128)(2,1)S(1)}, u32[]{:S(2)}, u32[]{:S(2)}) %all-to-all-start.2) | async-done | bytes 655392 | tf_op jit(solution)/shard_map/all_to_all | solution.py:287
  149.7 0.7 pad_maximum_fusion
  150.4 5.5 %all-to-all-start.3 = ((bf16[16,49,128]{2,1,0:T(8,128)(2,1)}), bf16[16,49,128]{2,1,0:T(8,128)(2,1)S(1)}, u32[]{:S(2)}, u32[]{:S(2)}) async-start(bf16[16,49,128]{2,1,0:T(8,128)(2,1)} %pad_maximum_fusion), calls=%async_computation.3 | async-start | bytes 458752 | tf_op jit(solution)/shard_map/all_to_all | solution.py:294
  155.9 3.7 %copy-done.8 = bf16[1152,4096]{1,0:T(8,128)(2,1)S(1)} copy-done((bf16[1152,4096]{1,0:T(8,128)(2,1)S(1)}, bf16[1152,4096]{1,0:T(8,128)(2,1)}, u32[]{:S(2)}) %copy-start.8) | copy-done | bytes 9437208
  159.6 6.1 %input_stage.1 = bf16[128,1152]{1,0:T(8,128)(2,1)} custom-call(bf16[128,4096]{1,0:T(8,128)(2,1)S(1)} %copy-done.7, bf16[8,4096]{1,0:T(8,128)(2,1)S(1)} %collective-permute-done.4.after_ref, bf16[4,4096]{1,0:T(4,128)(2,1)S(1)} %copy-done.5, bf16[1152,4096]{1,0:T(8,128)(2,1)S(1)} %copy-done.8, bf16[128,128]{1,0:T(8,128)(2,1)S(1)} %get-tuple-element.44.latent_ref, ...), custom_call_target="tpu_custom_call" | custom-call | flops 24159191040 | bytes 83886080 | tf_op jit(solution)/shard_map/input_stage/pallas_call | solution.py:189
  165.7 2.8 %all-to-all-done.3 = bf16[16,49,128]{2,1,0:T(8,128)(2,1)S(1)} async-done(((bf16[16,49,128]{2,1,0:T(8,128)(2,1)}), bf16[16,49,128]{2,1,0:T(8,128)(2,1)S(1)}, u32[]{:S(2)}, u32[]{:S(2)}) %all-to-all-start.3) | async-done | bytes 200736 | tf_op jit(solution)/shard_map/all_to_all | solution.py:294
  168.5 0.7 broadcast_in_dim.53
  169.1 6.8 %all-to-all-start.4 = ((f32[4,49,128]{2,1,0:T(8,128)}), f32[4,49,128]{2,1,0:T(8,128)S(1)}, u32[]{:S(2)}, u32[]{:S(2)}) async-start(f32[4,49,128]{2,1,0:T(8,128)} %broadcast_in_dim.53), calls=%async_computation.4 | async-start | bytes 229376 | tf_op jit(solution)/shard_map/all_to_all | solution.py:302
  175.9 4.4 %all-to-all-done.4.shares_ref = f32[4,49,128]{2,1,0:T(8,128)S(1)} async-done(((f32[4,49,128]{2,1,0:T(8,128)}), f32[4,49,128]{2,1,0:T(8,128)S(1)}, u32[]{:S(2)}, u32[]{:S(2)}) %all-to-all-start.4) | async-done | bytes 100384 | tf_op jit(solution)/shard_map/all_to_all | solution.py:302
  (49 shorter events, 2.1 us)
Async XLA Ops:
  7.2 63.6 %copy-start = (f32[4096]{0:T(1024)S(1)}, f32[4096]{0:T(1024)}, u32[]{:S(2)}) copy-start(f32[4096]{0:T(1024)} %param.16) | copy-start | bytes 49156
  7.2 1.2 copy-start.10
  7.2 148.7 %all-gather.3.cloned.1.call-start = ((), (), s32[]{:S(2)}) async-start(), calls=%async_computation.5 | async-start | bytes 10616832 | tf_op jit(solution)/shard_map/all_gather | solution.py:260
  9.5 7.5 %copy-start.11 = (bf16[16,4096]{1,0:T(8,128)(2,1)S(1)}, bf16[16,4096]{1,0:T(8,128)(2,1)}, u32[]{:S(2)}) copy-start(bf16[16,4096]{1,0:T(8,128)(2,1)} %param.15) | copy-start | bytes 393220
  9.5 7.7 %copy-start.12 = (bf16[144,128]{1,0:T(8,128)(2,1)S(1)}, bf16[144,128]{1,0:T(8,128)(2,1)}, u32[]{:S(2)}) copy-start(bf16[144,128]{1,0:T(8,128)(2,1)} %param.14) | copy-start | bytes 110596
  9.5 43.9 %all-to-all-start = ((bf16[8,512,128]{2,1,0:T(8,128)(2,1)}), bf16[8,512,128]{2,1,0:T(8,128)(2,1)S(1)}, u32[]{:S(2)}, u32[]{:S(2)}) async-start(bf16[8,512,128]{2,1,0:T(8,128)(2,1)} %bitcast.4), calls=%async_computation | async-start | bytes 2097152 | tf_op jit(solution)/shard_map/all_to_all | solution.py:256
  17.0 17.0 %copy-start.2 = (bf16[1,128,1152]{2,1,0:T(8,128)(2,1)S(1)}, bf16[1,128,1152]{2,1,0:T(8,128)(2,1)}, u32[]{:S(2)}) copy-start(bf16[1,128,1152]{2,1,0:T(8,128)(2,1)} %param.9) | copy-start | bytes 884740
  33.2 0.8 copy-start.9
  34.0 32.6 %copy-start.1 = (bf16[1,128,4096]{2,1,0:T(8,128)(2,1)S(1)}, bf16[1,128,4096]{2,1,0:T(8,128)(2,1)}, u32[]{:S(2)}) copy-start(bf16[1,128,4096]{2,1,0:T(8,128)(2,1)} %param.10) | copy-start | bytes 3145732
  53.4 1.0 copy-start.3
  54.4 61.6 %all-to-all-start.1 = ((bf16[32,128,128]{2,1,0:T(8,128)(2,1)}), bf16[32,128,128]{2,1,0:T(8,128)(2,1)S(1)}, u32[]{:S(2)}, u32[]{:S(2)}) async-start(bf16[32,128,128]{2,1,0:T(8,128)(2,1)} %bitcast.50), calls=%async_computation.1 | async-start | bytes 2097152 | tf_op jit(solution)/shard_map/all_to_all | solution.py:272
  66.6 49.3 %copy-start.5 = (bf16[4,4096]{1,0:T(4,128)(2,1)S(1)}, bf16[4,4096]{1,0:T(4,128)(2,1)}, u32[]{:S(2)}) copy-start(bf16[4,4096]{1,0:T(4,128)(2,1)} %taps_ref.3) | copy-start | bytes 98308
  66.6 34.5 %collective-permute-start.3 = (bf16[8,4096]{1,0:T(8,128)(2,1)S(1)}, bf16[8,4096]{1,0:T(8,128)(2,1)S(1)}, u32[]{:S(2)}, u32[]{:S(2)}) collective-permute-start(bf16[8,4096]{1,0:T(8,128)(2,1)S(1)} %slice_bitcast_fusion), channel_id=1, source_target_pairs={{0,16},{16,32},{32,48},{48,64},{64,80},{80,96},{96,112},{112,128},... | collective-permute-start | bytes 196616 | tf_op jit(solution)/shard_map/ppermute | solution.py:259
  70.8 1.2 copy-start.4
  73.2 52.6 %collective-permute-start = (bf16[128,128]{1,0:T(8,128)(2,1)S(1)}, bf16[128,128]{1,0:T(8,128)(2,1)S(1)}, u32[]{:S(2)}, u32[]{:S(2)}) collective-permute-start(bf16[128,128]{1,0:T(8,128)(2,1)S(1)} %get-tuple-element.30), channel_id=1, source_target_pairs={{0,128},{64,192},{128,0},{192,64},{1,129},{65,193},{129,1},{193,65... | collective-permute-start | bytes 98312 | tf_op jit(solution)/shard_map/ppermute | solution.py:242
  84.1 41.7 %collective-permute-start.1 = (bf16[128,128]{1,0:T(8,128)(2,1)S(1)}, bf16[128,128]{1,0:T(8,128)(2,1)S(1)}, u32[]{:S(2)}, u32[]{:S(2)}) collective-permute-start(bf16[128,128]{1,0:T(8,128)(2,1)S(1)} %get-tuple-element.31), channel_id=1, source_target_pairs={{0,64},{64,128},{128,192},{192,0},{1,65},{65,129},{129,193},{193,1... | collective-permute-start | bytes 98312 | tf_op jit(solution)/shard_map/ppermute | solution.py:242
  86.3 39.5 %collective-permute-start.2 = (bf16[128,128]{1,0:T(8,128)(2,1)S(1)}, bf16[128,128]{1,0:T(8,128)(2,1)S(1)}, u32[]{:S(2)}, u32[]{:S(2)}) collective-permute-start(bf16[128,128]{1,0:T(8,128)(2,1)S(1)} %get-tuple-element.32), channel_id=1, source_target_pairs={{0,192},{64,0},{128,64},{192,128},{1,193},{65,1},{129,65},{193,129... | collective-permute-start | bytes 98312 | tf_op jit(solution)/shard_map/ppermute | solution.py:242
  119.2 1.0 copy-start.6
  125.8 12.3 %copy-start.7 = (bf16[128,4096]{1,0:T(8,128)(2,1)S(1)}, bf16[128,4096]{1,0:T(8,128)(2,1)}, u32[]{:S(2)}) copy-start(bf16[128,4096]{1,0:T(8,128)(2,1)} %copy-done.6) | copy-start | bytes 3145732
  127.0 22.4 %all-to-all-start.2 = ((bf16[32,80,128]{2,1,0:T(8,128)(2,1)}), bf16[32,80,128]{2,1,0:T(8,128)(2,1)S(1)}, u32[]{:S(2)}, u32[]{:S(2)}) async-start(bf16[32,80,128]{2,1,0:T(8,128)(2,1)} %get-tuple-element.42), calls=%async_computation.2 | async-start | bytes 1310720 | tf_op jit(solution)/shard_map/all_to_all | solution.py:287
  138.1 17.7 %collective-permute-start.4 = (bf16[8,4096]{1,0:T(8,128)(2,1)S(1)}, bf16[8,4096]{1,0:T(8,128)(2,1)S(1)}, u32[]{:S(2)}, u32[]{:S(2)}) collective-permute-start(bf16[8,4096]{1,0:T(8,128)(2,1)S(1)} %slice.27), channel_id=1, source_target_pairs={{16,0},{32,16},{48,32},{64,48},{80,64},{96,80},{112,96},{128,112},... | collective-permute-start | bytes 196616 | tf_op jit(solution)/shard_map/ppermute | solution.py:286
  150.4 18.1 %all-to-all-start.3 = ((bf16[16,49,128]{2,1,0:T(8,128)(2,1)}), bf16[16,49,128]{2,1,0:T(8,128)(2,1)S(1)}, u32[]{:S(2)}, u32[]{:S(2)}) async-start(bf16[16,49,128]{2,1,0:T(8,128)(2,1)} %pad_maximum_fusion), calls=%async_computation.3 | async-start | bytes 458752 | tf_op jit(solution)/shard_map/all_to_all | solution.py:294
  155.9 3.7 %copy-start.8 = (bf16[1152,4096]{1,0:T(8,128)(2,1)S(1)}, bf16[1152,4096]{1,0:T(8,128)(2,1)}, u32[]{:S(2)}) copy-start(bf16[1152,4096]{1,0:T(8,128)(2,1)} %all-gather.3.cloned.1.call-done.key_ref) | copy-start | bytes 28311556
  169.1 11.2 %all-to-all-start.4 = ((f32[4,49,128]{2,1,0:T(8,128)}), f32[4,49,128]{2,1,0:T(8,128)S(1)}, u32[]{:S(2)}, u32[]{:S(2)}) async-start(f32[4,49,128]{2,1,0:T(8,128)} %broadcast_in_dim.53), calls=%async_computation.4 | async-start | bytes 229376 | tf_op jit(solution)/shard_map/all_to_all | solution.py:302
Sparse Core Ops, SparseCore 0:
  10.1 67.5 all-gather.2
